TPU v7x, 256 devices: a whole 4x4x8 slice. The times are simulated.
256 devices in a mesh: seq: 32 (over y, z), exp: 8 (over x, core).
Axes of the slice: x: 4, y: 4, z: 8, core: 2. Of those that a mesh axis runs over, the one named last changes fastest.
Arguments:
- residual_in: bfloat16 [4096, 4096], P('seq'), may hold values from -3 to 3
- mamba_in: bfloat16 [3, 4096, 8192], P(None, 'seq', 'exp'), may hold values from -6 to 6
- bc_proj: float32 [32, 4096], P(None, 'seq'), may hold values from -6 to 6
- decay: float32 [16, 8192], P(None, 'exp'), may hold values from 2.4414063e-05 to 0.08
- conv_w: float32 [4, 8192], P(None, 'exp'), may hold values from -3 to 3
- mamba_vec: float32 [3, 8192], P(None, 'exp'), may hold values from -1 to 1
- doc_len: int32 [8], replicated, may hold values from 1 to 2048, 4096 in all
- w_out: bfloat16 [8192, 4096], P('exp', 'seq'), may hold values from -0.0625 to 0.0625
- norm_gain: float32 [4096], replicated, may hold values from 0.1 to 1.9
- routes: int32 [4096, 2], P('seq'), may hold values from 0 to 7, all different within a row; in each aligned block of 128 rows (0 to 127, 128 to 255, ...) at most 36 rows name the same one
- gate_w: float32 [4096, 2], P('seq'), may hold values from 0.5 to 3
- w_gate_up: bfloat16 [8, 2, 4096, 12288], P('exp', None, None, 'seq'), may hold values from -0.09375 to 0.09375
- w_down: bfloat16 [8, 12288, 4096], P('exp', 'seq'), may hold values from -0.3125 to 0.3125
Outputs:
- layer_out: bfloat16 [4096, 4096], P('seq', 'exp')
Inputs may be any that keep to these rules, and one draw needn't show every extreme that they name: `routes`: in each aligned block of 128 rows no expert is named by more than 36 rows, a bound that some block reaches; the two experts of a row differ.
All inputs are finite; a program needn't handle non-finite values.
Results may differ from a plain program's by a relative error of at most 0.03.
Values may be sent and summed in bfloat16 or wider, within the bound.
A program may use at most 128 MiB of HBM per device.

v0:
```python
import jax
import jax.numpy as jnp
from jax import lax
from jax.sharding import PartitionSpec as P


def from_behind(value, axis, steps):
    count = lax.axis_size(axis)
    initial, last = (max(0, -steps), min(count, count - steps))
    return lax.ppermute(value, axis, [(source, source + steps) for source in range(initial, last)])


def document_index(positions, doc_len):
    ends = jnp.cumsum(doc_len)
    return jnp.sum((ends[None, :] <= positions[:, None]).astype(jnp.int32), axis=1)


def shards(
    residual_in,
    mamba_in,
    bc_proj,
    decay,
    conv_w,
    mamba_vec,
    doc_len,
    w_out,
    norm_gain,
    routes,
    gate_w,
    w_gate_up,
    w_down,
):
    tok_rows = mamba_in.shape[1]
    channels = mamba_in.shape[2]
    nstate = decay.shape[0]
    width = conv_w.shape[0]
    x_part = mamba_in[0]
    tail_rows = from_behind(x_part[tok_rows - (width - 1) :], "seq", 1)
    extended = jnp.concatenate([tail_rows, x_part], axis=0).astype(jnp.float32)
    first = lax.axis_index("seq") * tok_rows
    ext_positions = first - (width - 1) + jnp.arange(tok_rows + width - 1, dtype=jnp.int32)
    ext_docs = document_index(ext_positions, doc_len)
    docs = ext_docs[width - 1 :]
    total = jnp.zeros((tok_rows, channels), jnp.float32) + mamba_vec[0][None, :]
    for offset in range(width):
        valid = (
            (ext_positions[offset : offset + tok_rows] >= 0)
            & (ext_docs[offset : offset + tok_rows] == docs)
        ).astype(jnp.float32)
        total = (
            total + conv_w[offset][None, :] * extended[offset : offset + tok_rows] * valid[:, None]
        )
    u_values = jax.nn.silu(total)
    step_size = jax.nn.softplus(mamba_in[2].astype(jnp.float32) + mamba_vec[1][None, :])
    keep = (ext_docs[width - 2 : width - 2 + tok_rows] == docs).astype(jnp.float32)
    b_rows = bc_proj[:nstate].T
    c_rows = bc_proj[nstate:].T

    def advance(carried, inputs):
        state, cumul = carried
        dt_row, u_row, b_row, c_row, keep_row = inputs
        growth = jnp.exp(-dt_row[None, :] * decay) * keep_row
        state = growth * state + b_row[:, None] * (dt_row * u_row)[None, :]
        cumul = growth * cumul
        output = jnp.sum(state * c_row[:, None], axis=0)
        return ((state, cumul), (output, cumul * c_row[:, None]))

    start = (jnp.zeros((nstate, channels), jnp.float32), jnp.ones((nstate, channels), jnp.float32))
    (end_state, end_decay), (outputs, weighted) = lax.scan(
        advance, start, (step_size, u_values, b_rows, c_rows, keep)
    )

    def chain_step(iteration, incoming):
        return from_behind(
            (end_decay * incoming + end_state).astype(jnp.bfloat16), "seq", 1
        ).astype(jnp.float32)

    entering = lax.fori_loop(
        0, lax.axis_size("seq") - 1, chain_step, jnp.zeros((nstate, channels), jnp.float32)
    )
    correction = jnp.sum(weighted * entering[None, :, :], axis=1)
    mixer_y = outputs + correction + mamba_vec[2][None, :] * u_values
    gated = (mixer_y * jax.nn.silu(mamba_in[1].astype(jnp.float32))).astype(jnp.bfloat16)
    partial_mix = jnp.dot(
        gated, lax.all_gather(w_out, "seq", axis=1, tiled=True), preferred_element_type=jnp.float32
    )
    model_width = partial_mix.shape[1]
    slice_width = model_width // lax.axis_size("exp")
    part_index = lax.axis_index("exp")
    mix = lax.psum(partial_mix.astype(jnp.bfloat16), "exp").astype(jnp.float32)
    resid = residual_in.astype(jnp.float32) + mix
    mean_sq = jnp.mean(resid * resid, axis=1, keepdims=True)
    normed = (resid * lax.rsqrt(mean_sq + 1e-05) * norm_gain[None, :]).astype(jnp.bfloat16)
    resid_slice = lax.dynamic_slice_in_dim(resid, part_index * slice_width, slice_width, 1)
    capacity = tok_rows * 2 // lax.axis_size("exp") + max(tok_rows // 32, 1)
    expert_id = lax.axis_index("exp")
    flat_routes = routes.reshape(-1)
    hits = (flat_routes == expert_id).astype(jnp.int32)
    slots = jnp.cumsum(hits) - 1
    picked = (
        (slots[None, :] == jnp.arange(capacity, dtype=jnp.int32)[:, None]) & (hits[None, :] == 1)
    ).astype(jnp.float32)
    dispatch = jnp.sum(picked.reshape(capacity, tok_rows, 2), axis=2).astype(jnp.bfloat16)
    sent_rows = jnp.dot(dispatch, normed, preferred_element_type=jnp.float32).astype(jnp.bfloat16)
    weight_sel = jnp.sum(gate_w * (routes == expert_id).astype(jnp.float32), axis=1)
    piece = lax.all_gather(sent_rows, "seq", axis=0, tiled=True)
    gate_part = jnp.dot(piece, w_gate_up[0, 0], preferred_element_type=jnp.float32)
    up_part = jnp.dot(piece, w_gate_up[0, 1], preferred_element_type=jnp.float32)
    hidden = (jax.nn.silu(gate_part) * up_part).astype(jnp.bfloat16)
    expert_out = lax.psum_scatter(
        jnp.dot(hidden, w_down[0], preferred_element_type=jnp.float32).astype(jnp.bfloat16),
        "seq",
        scatter_dimension=0,
        tiled=True,
    )
    spread = jnp.dot(dispatch.T, expert_out, preferred_element_type=jnp.float32)
    moe = lax.psum_scatter(
        (weight_sel[:, None] * spread).astype(jnp.bfloat16), "exp", scatter_dimension=1, tiled=True
    ).astype(jnp.float32)
    return (resid_slice + moe).astype(jnp.bfloat16)


def solution(mesh):
    in_specs = (
        P("seq", None),
        P(None, "seq", "exp"),
        P(None, "seq"),
        P(None, "exp"),
        P(None, "exp"),
        P(None, "exp"),
        P(),
        P("exp", "seq"),
        P(),
        P("seq", None),
        P("seq", None),
        P("exp", None, None, "seq"),
        P("exp", "seq", None),
    )
    out_specs = P("seq", "exp")
    return jax.shard_map(shards, mesh=mesh, in_specs=in_specs, out_specs=out_specs, check_vma=False)
```

profile of v0, /device:TPU:1, one launch (start us, length us, event | category | flops | bytes accessed | tf_op | source)
XLA Modules:
  0.0 1456.2 jit_solution(17436268719033013226)
XLA Ops:
  6.5 1.5 slice_bitcast_fusion.1
  8.0 5.0 collective-permute-start.1
  13.1 1.7 slice_bitcast_fusion
  16.3 1.5 fusion.63
  17.8 1.4 fusion.61
  19.2 2.1 compare_select_fusion
  27.6 2.0 divide_multiply_fusion
  29.5 730.3 %while.30 = (s32[]{:T(128)}, f32[16,1024]{1,0:T(8,128)S(1)}, f32[16,1024]{1,0:T(8,128)S(1)}, f32[128,1024]{1,0:T(8,128)}, f32[128,16,1024]{2,1,0:T(8,128)}, /*in...) while((s32[]{:T(128)}, f32[16,1024]{1,0:T(8,128)S(1)}, ...), condition=%wide.region_4.5_spmd.clone.clone, body=%wide.region_2.4_spmd.clone.sunk.clone | while | flops 214019 | bytes 501332 | solution.py:69
  33.9 1.4 dynamic_update_slice.16
  39.6 1.4 dynamic_update_slice.16
  45.3 1.4 dynamic_update_slice.16
  68.2 1.4 dynamic_update_slice.16
  100.3 1.4 bitcast_dynamic-update-slice_fusion.3
  339.9 1.4 bitcast_dynamic-update-slice_fusion.3
  759.8 188.8 %while.31 = (s32[]{:T(128)}, f32[16,1024]{1,0:T(8,128)S(1)}, f32[16,1024]{1,0:T(8,128)S(1)}, f32[16,1024]{1,0:T(8,128)S(1)}) while((s32[]{:T(128)}, f32[16,1024]{1,0:T(8,128)S(1)}, f32[16,1024]{1,0:T(8,128)S(1)}, f32[16,1024]{1,0:T(8,128)S(1)}) %tuple.76), condition=%wide.region_6.7_spmd.clone.clone, body=%wide.region_5.6_spmd.clone.sunk.clone | while | flops 81923 | bytes 458855 | solution.py:78
  759.8 3.0 collective-permute-start
  763.8 3.6 collective-permute-start
  768.5 4.6 collective-permute-start
  774.2 3.6 collective-permute-start
  778.9 3.9 collective-permute-start
  783.8 4.9 collective-permute-start
  789.7 4.9 collective-permute-start
  795.6 4.9 collective-permute-start
  801.5 4.9 collective-permute-start
  807.4 5.3 collective-permute-start
  813.8 4.9 collective-permute-start
  819.7 4.9 collective-permute-start
  825.6 4.9 collective-permute-start
  831.6 4.7 collective-permute-start
  837.4 4.9 collective-permute-start
  843.2 4.9 collective-permute-start
  849.2 4.9 collective-permute-start
  855.1 4.9 collective-permute-start
  861.0 4.9 collective-permute-start
  866.9 5.3 collective-permute-start
  873.2 5.9 collective-permute-start
  880.2 6.0 collective-permute-start
  887.3 5.9 collective-permute-start
  894.2 5.6 collective-permute-start
  900.9 5.8 collective-permute-start
  907.6 5.9 collective-permute-start
  914.6 5.6 collective-permute-start
  921.2 5.8 collective-permute-start
  928.0 6.0 collective-permute-start
  935.1 5.8 collective-permute-start
  942.0 5.6 collective-permute-start
  948.7 6.2 multiply_reduce_fusion.1
  954.9 6.3 convolution_convert_fusion.1
  961.4 119.7 %all-reduce.4.cloned.1.call-done = bf16[128,4096]{1,0:T(8,128)(2,1)} async-done(((bf16[128,4096]{1,0:T(8,128)(2,1)}), bf16[128,4096]{1,0:T(8,128)(2,1)}) %all-reduce.4.cloned.1.call-update) | async-done | bytes 1048592 | tf_op jit(solution)/shard_map/psum | solution.py:90
  1081.1 3.4 convert_add_fusion
  1086.1 110.0 %all-gather.6.cloned.1.call-done = bf16[32,36,4096]{2,1,0:T(8,128)(2,1)} async-done(((bf16[1,36,4096]{2,1,0:T(8,128)(2,1)}), bf16[32,36,4096]{2,1,0:T(8,128)(2,1)}) %all-gather.6.cloned.1.call-update) | async-done | bytes 9437200 | tf_op jit(solution)/shard_map/all_gather | solution.py:106
  1196.1 13.2 reshape.115
  1209.3 9.5 fusion.10
  1218.8 15.8 %convolution_convert_fusion = bf16[1152,4096]{1,0:T(8,128)(2,1)} fusion(bf16[1,384,4096]{2,1,0:T(8,128)(2,1)S(1)} %copy-done, bf16[1152,4096]{1,0:T(8,128)(2,1)} %reshape.115, bf16[1,2,4096,384]{3,2,1,0:T(8,128)(2,1)} %param.28, f32[1152,384]{1,0:T(8,128)} %fusion.10), kind=kOutput, calls=%fused_computation.15 | convolution fusion | flops 7255130112 | bytes 26935296 | tf_op jit(solution)/shard_map/dot_general | solution.py:111
  1234.6 119.1 %fusion = bf16[40,4096]{1,0:T(8,128)(2,1)S(1)} fusion(bf16[1152,4096]{1,0:T(8,128)(2,1)} %convolution_convert_fusion), kind=kCustom, calls=%all-reduce-scatter | all-reduce-scatter fusion | flops 5242881 | bytes 9765888
  1353.7 2.0 collective-permute-start.2
  1355.7 2.5 collective-permute-start.3
  1358.2 4.0 collective-permute-start.4
  1362.3 4.2 collective-permute-start.5
  1369.2 10.1 collective-permute-done.5
  1379.3 13.3 concatenate.4
  1392.6 2.5 fusion.6
  1395.1 52.9 %reduce-scatter.4.cloned.1.call-done = bf16[128,512]{1,0:T(8,128)(2,1)} async-done(((bf16[128,4096]{1,0:T(8,128)(2,1)}), bf16[128,512]{1,0:T(8,128)(2,1)}) %reduce-scatter.4.cloned.1.call-update) | async-done | bytes 131088 | tf_op jit(solution)/shard_map/reduce_scatter | solution.py:117
  1448.0 1.7 add_convert_fusion
  (916 shorter events, 764.6 us)
Async XLA Ops:
  6.5 1212.3 %copy-start = (bf16[1,384,4096]{2,1,0:T(8,128)(2,1)S(1)}, bf16[1,384,4096]{2,1,0:T(8,128)(2,1)}, u32[]{:S(2)}) copy-start(bf16[1,384,4096]{2,1,0:T(8,128)(2,1)} %param.29) | copy-start | bytes 9437188
  6.5 23.0 %copy-start.1 = (f32[16,1024]{1,0:T(8,128)S(1)}, f32[16,1024]{1,0:T(8,128)}, u32[]{:S(2)}) copy-start(f32[16,1024]{1,0:T(8,128)} %param.20) | copy-start | bytes 196612
  6.5 948.3 %all-gather.4.cloned.1.call-start = ((), (), s32[]{:S(2)}) async-start(), calls=%async_computation.1 | async-start | bytes 8650752 | tf_op jit(solution)/shard_map/all_gather | solution.py:85
  8.0 18.5 %collective-permute-start.1 = (bf16[3,1024]{1,0:T(4,128)(2,1)}, bf16[3,1024]{1,0:T(4,128)(2,1)}, u32[]{:S(2)}, u32[]{:S(2)}) collective-permute-start(bf16[3,1024]{1,0:T(4,128)(2,1)} %slice_bitcast_fusion.1), channel_id=1, source_target_pairs={{0,8},{8,16},{16,24},{24,32},{32,40},{40,48},{48,56},{56,64},{64,7... | collective-permute-start | bytes 18440 | tf_op jit(solution)/shard_map/ppermute | solution.py:10
  13.0 1068.1 %all-reduce.4.cloned.1.call-start = ((), (), s32[]{:S(2)}) async-start(), calls=%async_computation.2 | async-start | bytes 2097152 | tf_op jit(solution)/shard_map/psum | solution.py:90
  24.9 4.6 copy-start.6
  759.8 4.0 collective-permute-start
  763.8 4.7 collective-permute-start
  768.5 5.7 collective-permute-start
  774.2 4.7 collective-permute-start
  778.9 4.9 collective-permute-start
  783.8 5.9 collective-permute-start
  789.7 5.9 collective-permute-start
  795.6 5.9 collective-permute-start
  801.5 5.9 collective-permute-start
  807.4 6.3 collective-permute-start
  813.8 5.9 collective-permute-start
  819.7 5.9 collective-permute-start
  825.6 6.1 collective-permute-start
  831.6 5.7 collective-permute-start
  837.4 5.9 collective-permute-start
  843.2 5.9 collective-permute-start
  849.2 5.9 collective-permute-start
  855.1 5.9 collective-permute-start
  861.0 5.9 collective-permute-start
  866.9 6.3 collective-permute-start
  873.2 7.0 collective-permute-start
  880.2 7.0 collective-permute-start
  887.3 7.0 collective-permute-start
  894.2 6.6 collective-permute-start
  900.9 6.8 collective-permute-start
  907.6 6.9 collective-permute-start
  914.6 6.7 collective-permute-start
  921.2 6.8 collective-permute-start
  928.0 7.0 collective-permute-start
  935.1 6.9 collective-permute-start
  942.0 6.6 collective-permute-start
  948.7 6.2 copy-start.4
  954.9 6.4 copy-start.5
  961.2 123.2 %copy-start.7 = (f32[4096]{0:T(1024)S(1)}, f32[4096]{0:T(1024)}, u32[]{:S(2)}) copy-start(f32[4096]{0:T(1024)} %param.25) | copy-start | bytes 49156
  961.2 234.9 %all-gather.6.cloned.1.call-start = ((), (), s32[]{:S(2)}) async-start(), calls=%async_computation.4 | async-start | bytes 10813440 | tf_op jit(solution)/shard_map/all_gather | solution.py:106
  1081.1 3.4 copy-start.2
  1081.1 3.4 copy-start.3
  1085.8 362.1 %reduce-scatter.4.cloned.1.call-start = ((), (), s32[]{:S(2)}) async-start(), calls=%async_computation.3 | async-start | bytes 1179648 | tf_op jit(solution)/shard_map/reduce_scatter | solution.py:117
  1353.7 25.6 %collective-permute-start.2 = (bf16[40,4096]{1,0:T(8,128)(2,1)S(1)}, bf16[40,4096]{1,0:T(8,128)(2,1)}, u32[]{:S(2)}, u32[]{:S(2)}) collective-permute-start(bf16[40,4096]{1,0:T(8,128)(2,1)S(1)} %fusion), channel_id=1, source_target_pairs={{0,8},{8,16},{16,24},{24,32},{32,40},{40,48},{48,56},{56,64},{64,7... | collective-permute-start | bytes 983048
  1355.7 23.6 %collective-permute-start.3 = (bf16[40,4096]{1,0:T(8,128)(2,1)S(1)}, bf16[40,4096]{1,0:T(8,128)(2,1)}, u32[]{:S(2)}, u32[]{:S(2)}) collective-permute-start(bf16[40,4096]{1,0:T(8,128)(2,1)S(1)} %fusion), channel_id=1, source_target_pairs={{0,16},{8,24},{16,32},{24,40},{32,48},{40,56},{48,64},{56,72},{64,... | collective-permute-start | bytes 983048
  1358.2 21.0 %collective-permute-start.4 = (bf16[40,4096]{1,0:T(8,128)(2,1)S(1)}, bf16[40,4096]{1,0:T(8,128)(2,1)}, u32[]{:S(2)}, u32[]{:S(2)}) collective-permute-start(bf16[40,4096]{1,0:T(8,128)(2,1)S(1)} %fusion), channel_id=1, source_target_pairs={{0,24},{8,32},{16,40},{24,48},{32,56},{40,64},{48,72},{56,80},{64,... | collective-permute-start | bytes 983048
  1362.3 17.0 %collective-permute-start.5 = (bf16[4,4096]{1,0:T(4,128)(2,1)S(1)}, bf16[4,4096]{1,0:T(4,128)(2,1)S(1)}, u32[]{:S(2)}, u32[]{:S(2)}) collective-permute-start(bf16[4,4096]{1,0:T(4,128)(2,1)S(1)} %slice.128), channel_id=1, source_target_pairs={{0,32},{8,40},{16,48},{24,56},{32,64},{40,72},{48,80},{56,88},{64,... | collective-permute-start | bytes 98312
Sparse Core Ops, SparseCore 0:
  13.1 102.2 all-gather.3
  961.4 119.6 all-reduce.3
  1086.0 110.0 all-gather.5
  1395.2 52.7 reduce-scatter.3
where the time goes:
time: 1480 us; the launch traced here: 1460 us
  other arithmetic  398 us (27%)
  local copies, waits for them, and re-layouts  389 us (26%)
  waiting for transfers between devices  324 us (22%)
  starting transfers between devices  174 us (12%)
  blocking collectives  119 us (8%)
  matrix products  35.4 us (2%)
    dynamic_update_slice x128, local copies, waits for them, and re-layouts, shards(): lax.scan(advance, start, (step_size, u_values, b_rows, c_rows, keep))  177 us
    dynamic_update_slice x128, other arithmetic, shards(): lax.scan(advance, start, (step_size, u_values, b_rows, c_rows, keep))  177 us
    ppermute x32, starting transfers between devices, from_behind(): lax.ppermute(value, axis, [(source, source + steps) for source in range(i...  161 us
    psum x1, waiting for transfers between devices, shards(): mix = lax.psum(partial_mix.astype(jnp.bfloat16), 'exp').astype(jnp.float32)  120 us
    unnamed x1, blocking collectives  119 us
    all_gather x1, waiting for transfers between devices, shards(): piece = lax.all_gather(sent_rows, 'seq', axis=0, tiled=True)  110 us
    neg x128, other arithmetic, advance(): growth = jnp.exp(-dt_row[None, :] * decay) * keep_row  101 us
    reduce_sum x128, other arithmetic, advance(): output = jnp.sum(state * c_row[:, None], axis=0)  99.4 us
  transfers between devices with their start and end apart: 40, of which 35 were waited for; matrix products, arithmetic and copies ran while one was open for 52% of the time, Pallas kernels for 0%

commit v1 on v0

v1 whole, which is shorter than its diff:
```python
import functools

import jax
import jax.numpy as jnp
from jax import lax
from jax.experimental import pallas as pl
from jax.experimental.pallas import tpu as pltpu
from jax.sharding import PartitionSpec as P

MESH = pl.DeviceIdType.MESH
LOG2E = 1.4426950408889634
LANES = 128
F32 = jnp.float32
BF16 = jnp.bfloat16
YS, ZS = 4, 8
CORES = 2
SLAB = 48
CAP_MAIN = 32

Y_OFFSETS = (0, 1, -1, 2)
Z_OFFSETS = (0, 1, -1, 2, -2, 3, -3, 4)
SLOTS = [(dy, dz) for dz in Z_OFFSETS for dy in Y_OFFSETS]
GROUP = 8


def far_steps(offset, size):
    top = size // 2
    if offset == 0:
        return [(1, 1, None), (-1, -1, None)]
    if offset == top:
        return []
    if offset > 0:
        return [(offset + 1, 1, 0 if offset + 1 == top else None)]
    return [(offset - 1, -1, None)] if offset - 1 > -top else [(top, -1, 1)]


def messages():
    found = []
    for tree in range(2):
        for dy, dz in SLOTS:
            if tree == 1 or dz == 0:
                for to, way, part in far_steps(dy, YS):
                    found.append((tree, (dy, dz), (to, dz), part, ("y", way)))
            if tree == 0 or dy == 0:
                for to, way, part in far_steps(dz, ZS):
                    found.append((tree, (dy, dz), (dy, to), part, ("z", way)))
    return found


MESSAGES = messages()
DEPTH = {slot: abs(slot[0]) + abs(slot[1]) for slot in SLOTS}
DEEPEST = max(DEPTH.values())


ORDER = [
    1, 2, 39, 40, 37, 38, 3, 4, -1, 5, 6, 7, -2, 8, -39, 43, 44, 45, -40, 50, -37, 41, -38, 42, 9,
    10, 48, 49, -3, -4, -5, -8, 13, 17, -6, -7, -43, 46, -44, 47, -45, 55, -50, 60, 53, 54, -41,
    -42, 11, 12, -48, 51, -49, 52, -9, -10, 14, 18, 58, 59, -13, -17, -46, -47, -55, 65, -60, 70,
    -53, 56, -54, 57, 15, 19, 63, 64, 21, 25, -11, -12, -51, -52, 16, 20, -58, 61, -59, 62, -14,
    -18, 68, 69, -65, -70, 22, 26, -56, -57, -15, -19, 23, 27, -63, 66, -64, 67, -21, -25, 29, 33,
    73, 74, -16, 24, -20, 28, -61, -62, -22, 30, -26, 34, -68, 71, -69, 72, -23, 31, -27, 35, -24,
    32, -28, 36, -73, 75, -74, 76, -66, -67, -29, -33, -30, -34, -71, -72, -31, -35, -32, -36, -75,
    -76,
]


def groups_full_at(at):
    last = {}
    for place, item in enumerate(ORDER):
        if item < 0:
            last[SLOTS.index(MESSAGES[-item - 1][2]) // GROUP] = place
    return [group for group in sorted(last) if last[group] == at]


def silu(v):
    return v / (1.0 + jnp.exp(-v))


def seq_id(index):
    return {"seq": index}


def exp_id(index):
    return {"exp": index}


def neighbour(axis, way):
    me = lax.axis_index("seq")
    y, z = me // ZS, me % ZS
    if axis == "y":
        return ((y + way + YS) % YS) * ZS + z
    return y * ZS + (z + way + ZS) % ZS


def spread(view, send_sems, recv_sems):
    def copy(k):
        tree, source, target, part, way = MESSAGES[k]
        return pltpu.make_async_remote_copy(
            src_ref=view(tree, SLOTS.index(source), part),
            dst_ref=view(tree, SLOTS.index(target), part),
            send_sem=send_sems.at[k],
            recv_sem=recv_sems.at[k],
            device_id=seq_id(neighbour(*way)),
            device_id_type=MESH,
        )

    def run(when_full, start=0, stop=len(ORDER)):
        for at in range(start, stop):
            item = ORDER[at]
            if item > 0:
                copy(item - 1).start()
            else:
                copy(-item - 1).wait_recv()
                for group in groups_full_at(at):
                    when_full(group)

    def finish():
        for k in range(len(MESSAGES)):
            copy(k).wait_send()

    return run, finish


def gather_sum(view, landing, add, send_sems, recv_sems):
    def copy(k):
        tree, _, child, part, (axis, way) = MESSAGES[k]
        return pltpu.make_async_remote_copy(
            src_ref=view(tree, SLOTS.index(child), part),
            dst_ref=landing(tree, SLOTS.index(child), part),
            send_sem=send_sems.at[k],
            recv_sem=recv_sems.at[k],
            device_id=seq_id(neighbour(axis, -way)),
            device_id_type=MESH,
        )

    def run():
        for item in reversed(ORDER):
            k = abs(item) - 1
            if item < 0:
                copy(k).start()
            else:
                copy(k).wait_recv()
                _, parent, child, part, _ = MESSAGES[k]
                add(MESSAGES[k][0], SLOTS.index(parent), SLOTS.index(child), part)

    def finish():
        for k in range(len(MESSAGES)):
            copy(k).wait_send()

    return run, finish


def dot(a, b):
    return jnp.dot(a, b, preferred_element_type=F32)


def one_hot(condition):
    return condition.astype(F32).astype(BF16)


def slot_table(routes):
    toks = routes.shape[0]
    expert = lax.broadcasted_iota(jnp.int32, (toks, LANES), 1)
    hits = jnp.logical_or(routes[:, 0:1] == expert, routes[:, 1:2] == expert)
    row = lax.broadcasted_iota(jnp.int32, (toks, toks), 0)
    col = lax.broadcasted_iota(jnp.int32, (toks, toks), 1)
    places = dot(one_hot(col <= row), one_hot(hits)) - 1.0
    return jnp.where(hits, places, -1.0)


def places_of(table_t, expert):
    place = lax.broadcasted_iota(jnp.int32, (SLAB, table_t.shape[1]), 0).astype(F32)
    return (place == table_t[expert : expert + 1, :]).astype(F32)


def split_lanes(width):
    first = (width * 13 // 32) // LANES * LANES
    quarter = width // 4
    rest = (quarter * 13 // 32) // LANES * LANES
    return (first, width - first), (rest, quarter - rest)


CHUNKS = 4
SHARES = [6, 12, 16, 22, 28, 34, 40, 46, 52, 60]


def mixer_kernel(
    reach,
    mamba_ref,
    bc_ref,
    decay_ref,
    conv_ref,
    vec_ref,
    doc_ref,
    residual_ref,
    w_ref,
    gain_ref,
    routes_ref,
    resid_ref,
    own_a,
    own_b,
    xs,
    dts,
    us,
    zs,
    neg,
    tail,
    end_out,
    end_in,
    sum_out,
    sum_in,
    held_a,
    held_b,
    gated,
    partial,
    pair_in,
    pair_sum,
    cross_in,
    disp,
    disp_in,
    squares,
    rows_n,
    send_sems,
    recv_sems,
    w_send_sems,
    w_recv_sems,
    exp_send_sems,
    exp_recv_sems,
):
    count = lax.axis_size("seq")
    me = lax.axis_index("seq")
    toks = mamba_ref.shape[1]
    blocks = mamba_ref.shape[2] // LANES
    nstate = decay_ref.shape[0]
    rows = blocks
    first = me * toks
    e = lax.axis_index("exp")
    experts_count = lax.axis_size("exp")
    x, core = e // CORES, e % CORES
    xs_count = experts_count // CORES

    barrier = pltpu.get_barrier_semaphore()

    def greet(step, _):
        pl.semaphore_signal(
            barrier, inc=1, device_id=seq_id(lax.rem(me + step, count)), device_id_type=MESH
        )
        return 0

    lax.fori_loop(1, count, greet, 0)
    for step in range(1, experts_count):
        pl.semaphore_signal(
            barrier,
            inc=1,
            device_id=exp_id(lax.rem(e + step, experts_count)),
            device_id_type=MESH,
        )

    depth = w_ref.shape[0]
    upper = held_a.shape[1]
    held_a[0] = w_ref[pl.ds(0, upper), :]
    held_b[0] = w_ref[pl.ds(upper, depth - upper), :]
    for j in range(blocks):
        lanes = pl.ds(j * LANES, LANES)
        xs[pl.ds(8 * rows + j, toks, stride=rows), :] = mamba_ref[0, :, lanes].astype(F32)
        zs[pl.ds(j, toks, stride=rows), :] = mamba_ref[1, :, lanes].astype(F32)
        dts[pl.ds(j, toks, stride=rows), :] = mamba_ref[2, :, lanes].astype(F32)
    pl.semaphore_wait(barrier, count - 1 + experts_count - 1)

    def held_view(tree, slot, part):
        ref = (held_a, held_b)[tree]
        size = ref.shape[1]
        if part is None:
            return ref.at[slot]
        return ref.at[slot, pl.ds(part * (size // 2), size // 2)]

    gather, gather_end = spread(held_view, w_send_sems, w_recv_sems)
    tail_copy = pltpu.make_async_remote_copy(
        src_ref=mamba_ref.at[0, pl.ds(toks - 16, 16)],
        dst_ref=tail,
        send_sem=send_sems.at[0],
        recv_sem=recv_sems.at[0],
        device_id=seq_id(lax.rem(me + 1, count)),
        device_id_type=MESH,
    )
    tail_copy.start()

    waiting = []
    reached = [0]

    def product(group):
        for pair in range(GROUP // 2):
            first_slot = group * GROUP + 2 * pair
            sides = [
                jnp.concatenate([held_a[first_slot + n], held_b[first_slot + n]], axis=0)
                for n in range(2)
            ]
            made = dot(gated[...], jnp.concatenate(sides, axis=1)).astype(BF16)
            for n in range(2):
                dy, dz = SLOTS[first_slot + n]
                y, z = me // ZS, me % ZS
                owner = ((y - dy + YS) % YS) * ZS + (z - dz + ZS) % ZS
                block = owner // tiles_per
                lane = pl.multiple_of((owner % tiles_per) * LANES, LANES)
                partial[block % CORES, block // CORES, :, pl.ds(lane, LANES)] = made[
                    :, n * LANES : (n + 1) * LANES
                ]

    tiles_per = resid_ref.shape[1] // LANES

    def forward(share, act=False):
        stop = len(ORDER) * share // 100
        gather(product if act else waiting.append, reached[0], stop)
        reached[0] = stop

    forward(SHARES[0])
    neg[...] = decay_ref[...] * (-LOG2E)
    step_bias = vec_ref[1]

    def tok(t):
        return pl.ds(pl.multiple_of(t * rows, rows), rows)

    def prepare(t, total):
        raw = dts[tok(t), :] + step_bias
        step = jnp.maximum(raw, 0.0) + jnp.log1p(jnp.exp(-jnp.abs(raw)))
        dts[tok(t), :] = step
        zs[tok(t), :] = silu(zs[tok(t), :])
        return total + step

    total_step = lax.fori_loop(0, toks, prepare, jnp.zeros((rows, LANES), F32), unroll=8)

    forward(SHARES[1])
    tail_copy.wait()
    there = jnp.where(me > 0, 1.0, 0.0).astype(F32)
    for j in range(blocks):
        rest = tail[:, pl.ds(j * LANES, LANES)].astype(F32) * there
        xs[pl.ds(j, 8, stride=rows), :] = rest[8:16, :]

    ends = []
    so_far = jnp.int32(0)
    for j in range(doc_ref.shape[0]):
        so_far = so_far + doc_ref[j]
        ends.append(so_far)

    def goes_on(position):
        keep = jnp.float32(1.0)
        for end in ends:
            keep = jnp.where(end == position, jnp.float32(0.0), keep)
        return keep

    taps = [conv_ref[k] for k in range(conv_ref.shape[0])]
    conv_bias = vec_ref[0]

    def advance(t, states, keep, step, drive):
        new = []
        for n in range(nstate):
            growth = jnp.exp2(step * neg[n]) * keep
            new.append(growth * states[n] + drive * bc_ref[n, t])
        return tuple(new)

    def local_pass(t, carry):
        states, before, before2 = carry
        keep = goes_on(first + t)
        x0, x1, x2, x3 = [xs[tok(t + 8 - 3 + k), :] for k in range(4)]
        v2 = keep
        v1 = keep * before
        v0 = v1 * before2
        total = conv_bias + (taps[0] * x0) * v0 + (taps[1] * x1) * v1
        total = total + (taps[2] * x2) * v2 + taps[3] * x3
        u_row = silu(total)
        us[tok(t), :] = u_row
        step = dts[tok(t), :]
        return advance(t, states, keep, step, step * u_row), keep, before

    zero = tuple(jnp.zeros((rows, LANES), F32) for _ in range(nstate))
    carry = (zero, goes_on(first - 1), goes_on(first - 2))
    for i in range(CHUNKS):
        carry = lax.fori_loop(
            i * toks // CHUNKS, (i + 1) * toks // CHUNKS, local_pass, carry, unroll=2
        )
        if i < CHUNKS - 1:
            forward(SHARES[2 + i])
    states = carry[0]
    for n in range(0, nstate, 2):
        pair = jnp.concatenate([states[n], states[n + 1]], axis=0)
        end_out[pl.ds(n * rows, 2 * rows), :] = pair.astype(BF16)
    sum_out[...] = total_step

    def copies(k):
        target = seq_id(lax.rem(me + k, count))
        one = pltpu.make_async_remote_copy(
            src_ref=end_out,
            dst_ref=end_in.at[k - 1],
            send_sem=send_sems.at[2 * k - 1],
            recv_sem=recv_sems.at[2 * k - 1],
            device_id=target,
            device_id_type=MESH,
        )
        two = pltpu.make_async_remote_copy(
            src_ref=sum_out,
            dst_ref=sum_in.at[k - 1],
            send_sem=send_sems.at[2 * k],
            recv_sem=recv_sems.at[2 * k],
            device_id=target,
            device_id_type=MESH,
        )
        return one, two

    def send(k, _):
        one, two = copies(k)
        one.start()
        two.start()
        return 0

    lax.fori_loop(1, reach + 1, send, 0)

    forward(SHARES[1 + CHUNKS])

    def finish(k, _):
        one, two = copies(k)
        one.wait()
        two.wait()
        return 0

    lax.fori_loop(1, reach + 1, finish, 0)

    def enter(i, states):
        k = reach - i
        source = me - k
        whole = jnp.where(source >= 0, jnp.float32(1.0), jnp.float32(0.0))
        start = source * toks
        unbroken = whole
        for end in ends:
            inside = jnp.logical_and(end >= start, end < start + toks)
            unbroken = jnp.where(inside, jnp.float32(0.0), unbroken)
        sums = sum_in[k - 1]
        new = []
        for n in range(0, nstate, 2):
            pair = end_in[k - 1, pl.ds(n * rows, 2 * rows), :].astype(F32)
            for m in range(2):
                growth = jnp.exp2(sums * neg[n + m]) * unbroken
                new.append(growth * states[n + m] + whole * pair[m * rows : (m + 1) * rows, :])
        return tuple(new)

    entering = lax.fori_loop(0, reach, enter, zero)
    forward(SHARES[2 + CHUNKS])
    skip = vec_ref[2]

    def full_pass(t, states):
        keep = goes_on(first + t)
        u_row = us[tok(t), :]
        step = dts[tok(t), :]
        states = advance(t, states, keep, step, step * u_row)
        total = skip * u_row
        for n in range(nstate):
            total = total + states[n] * bc_ref[nstate + n, t]
        zs[tok(t), :] = zs[tok(t), :] * total
        return states

    states = entering
    for i in range(CHUNKS):
        states = lax.fori_loop(
            i * toks // CHUNKS, (i + 1) * toks // CHUNKS, full_pass, states, unroll=2
        )
        if i < CHUNKS - 1:
            forward(SHARES[3 + CHUNKS + i])
    for j in range(blocks):
        gated[:, pl.ds(j * LANES, LANES)] = zs[pl.ds(j, toks, stride=rows), :].astype(BF16)
    for group in waiting:
        product(group)
    routes = routes_ref[...]
    table_t = slot_table(routes).T
    forward(100, act=True)

    def pair_copy(k):
        to = lax.rem(x + k, xs_count)
        return pltpu.make_async_remote_copy(
            src_ref=partial.at[1 - core, to],
            dst_ref=pair_in.at[to],
            send_sem=exp_send_sems.at[k],
            recv_sem=exp_recv_sems.at[k],
            device_id=exp_id(x * CORES + 1 - core),
            device_id_type=MESH,
        )

    def cross_copy(k):
        to = lax.rem(x + k, xs_count)
        return pltpu.make_async_remote_copy(
            src_ref=pair_sum.at[to],
            dst_ref=cross_in.at[k - 1],
            send_sem=exp_send_sems.at[xs_count + k],
            recv_sem=exp_recv_sems.at[xs_count + k],
            device_id=exp_id(to * CORES + core),
            device_id_type=MESH,
        )

    order = [2, 1, 3, 0]
    for k in order:
        pair_copy(k).start()
    for k in order:
        pair_copy(k).wait_recv()
        to = lax.rem(x + k, xs_count)
        total = partial[core, to].astype(F32) + pair_in[to].astype(F32)
        if k > 0:
            pair_sum[to] = total.astype(BF16)
            cross_copy(k).start()
    width = residual_ref.shape[1]
    block = width // experts_count
    total = total + residual_ref[:, pl.ds(pl.multiple_of(e * block, block), block)].astype(F32)
    for k in (1, 3, 2):
        cross_copy(k).wait_recv()
        total = total + cross_in[k - 1].astype(F32)
    resid_ref[...] = total

    square = jnp.sum(total * total, axis=1, keepdims=True)
    squares[e] = (square * jnp.ones((1, LANES), F32)).T[0:8, :]
    sent_rows = total.astype(BF16)
    for j in range(experts_count):
        disp[j] = dot(places_of(table_t, j).astype(BF16), sent_rows).astype(BF16)

    def deal(k):
        to = lax.rem(e + k, experts_count)
        base = 2 * xs_count + 2 * (k - 1)
        return [
            pltpu.make_async_remote_copy(
                src_ref=source,
                dst_ref=target,
                send_sem=exp_send_sems.at[base + i],
                recv_sem=exp_recv_sems.at[base + i],
                device_id=exp_id(to),
                device_id_type=MESH,
            )
            for i, (source, target) in enumerate(
                [(disp.at[to], disp_in.at[e]), (squares.at[e], squares.at[e])]
            )
        ]

    for k in range(1, experts_count):
        for copy in deal(k):
            copy.start()
    disp_in[e] = disp[e]
    expert_row = lax.broadcasted_iota(jnp.int32, (LANES, toks), 0)
    place_t = jnp.sum(jnp.where(expert_row == e, table_t, 0.0), axis=0, keepdims=True)
    at = lax.broadcasted_iota(jnp.int32, (SLAB, toks), 0).astype(F32)
    mine = (at == place_t).astype(F32)
    for k in range(1, experts_count):
        for copy in deal(k):
            copy.wait_recv()
    mean = squares[0]
    for j in range(1, experts_count):
        mean = mean + squares[j]
    inverse = lax.rsqrt(mean * (1.0 / width) + 1e-05)
    scale = jnp.sum(mine * inverse[0:1, :], axis=1, keepdims=True)
    for j in range(experts_count):
        here = pl.ds(j * block, block)
        rows_n[:, here] = (disp_in[j].astype(F32) * scale * gain_ref[:, here]).astype(BF16)
    mains, rests = split_lanes(width)
    quarter = width // 4
    small_row = lax.broadcasted_iota(jnp.int32, (16, 16), 0)
    small_col = lax.broadcasted_iota(jnp.int32, (16, 16), 1)
    packed = jnp.zeros((16, quarter), F32)
    for q in range(4):
        choose = one_hot(jnp.logical_and(small_col < 4, small_row == q * 4 + small_col))
        packed = packed + dot(choose, rows_n[pl.ds(CAP_MAIN, 16), pl.ds(q * quarter, quarter)])
    packed = packed.astype(BF16)
    start = 0
    rest_start = 0
    for tree, own in enumerate((own_a, own_b)):
        wide = mains[tree]
        for tile in range(2):
            own[:, pl.ds(tile * wide, wide)] = rows_n[pl.ds(tile * 16, 16), pl.ds(start, wide)]
        own[:, pl.ds(2 * wide, rests[tree])] = packed[:, rest_start : rest_start + rests[tree]]
        start += wide
        rest_start += rests[tree]

    gather_end()
    for k in range(xs_count):
        pair_copy(k).wait_send()
        if k > 0:
            cross_copy(k).wait_send()
    for k in range(1, experts_count):
        for copy in deal(k):
            copy.wait_send()


def mixer(mamba_in, bc_proj, decay, conv_w, mamba_vec, doc_len, residual, w_out, gain, routes):
    toks, channels = mamba_in.shape[1:]
    nstate = decay.shape[0]
    rows = channels // LANES
    reach = 2048 // toks
    width = residual.shape[1]
    count = lax.axis_size("exp")
    block = width // count
    depth = w_out.shape[0]
    upper = depth * 13 // 32 // 32 * 32
    mains, rests = split_lanes(width)
    sizes = [2 * main + rest for main, rest in zip(mains, rests)]
    xs_count = count // CORES
    exp_sems = 2 * xs_count + 2 * (count - 1)
    tiles = lambda a: a.reshape(a.shape[0], rows, LANES)
    vmem = pl.BlockSpec(memory_space=pltpu.VMEM)
    smem = pl.BlockSpec(memory_space=pltpu.SMEM)
    return pl.pallas_call(
        functools.partial(mixer_kernel, reach),
        out_shape=[jax.ShapeDtypeStruct((toks, block), F32)]
        + [jax.ShapeDtypeStruct((16, size), BF16) for size in sizes],
        in_specs=[vmem, smem, vmem, vmem, vmem, smem, vmem, vmem, vmem, vmem],
        out_specs=[vmem] * 3,
        scratch_shapes=[
            pltpu.VMEM(((toks + 8) * rows, LANES), F32),
            pltpu.VMEM((toks * rows, LANES), F32),
            pltpu.VMEM((toks * rows, LANES), F32),
            pltpu.VMEM((toks * rows, LANES), F32),
            pltpu.VMEM((nstate, rows, LANES), F32),
            pltpu.VMEM((16, channels), BF16),
            pltpu.VMEM((nstate * rows, LANES), BF16),
            pltpu.VMEM((reach, nstate * rows, LANES), BF16),
            pltpu.VMEM((rows, LANES), F32),
            pltpu.VMEM((reach, rows, LANES), F32),
            pltpu.VMEM((len(SLOTS), upper, LANES), BF16),
            pltpu.VMEM((len(SLOTS), depth - upper, LANES), BF16),
            pltpu.VMEM((toks, channels), BF16),
            pltpu.VMEM((CORES, xs_count, toks, block), BF16),
            pltpu.VMEM((xs_count, toks, block), BF16),
            pltpu.VMEM((xs_count, toks, block), BF16),
            pltpu.VMEM((xs_count - 1, toks, block), BF16),
            pltpu.VMEM((count, SLAB, block), BF16),
            pltpu.VMEM((count, SLAB, block), BF16),
            pltpu.VMEM((count, 8, LANES), F32),
            pltpu.VMEM((SLAB, width), BF16),
            pltpu.SemaphoreType.DMA((2 * reach + 1,)),
            pltpu.SemaphoreType.DMA((2 * reach + 1,)),
            pltpu.SemaphoreType.DMA((len(MESSAGES),)),
            pltpu.SemaphoreType.DMA((len(MESSAGES),)),
            pltpu.SemaphoreType.DMA((exp_sems,)),
            pltpu.SemaphoreType.DMA((exp_sems,)),
        ],
        compiler_params=pltpu.CompilerParams(
            collective_id=1, has_side_effects=True, vmem_limit_bytes=56 * 1024 * 1024
        ),
        name="mixer",
    )(
        mamba_in,
        bc_proj,
        tiles(decay),
        tiles(conv_w),
        tiles(mamba_vec),
        doc_len,
        residual,
        w_out,
        gain.reshape(1, width),
        routes,
    )


def experts_kernel(
    own_a,
    own_b,
    resid_ref,
    routes_ref,
    gate_ref,
    w1_ref,
    w2_ref,
    out_ref,
    held_a,
    held_b,
    outs_a,
    outs_b,
    sums_a,
    sums_b,
    w1,
    w2,
    rows_x,
    acc,
    hidden,
    few_acc,
    made_rows,
    sent,
    got,
    local_sems,
    send_sems,
    recv_sems,
    sum_send_sems,
    sum_recv_sems,
    out_send_sems,
    out_recv_sems,
):
    units, width = w2_ref.shape
    quarter = width // 4
    mains, rests = split_lanes(width)
    e = lax.axis_index("exp")
    count = lax.axis_size("exp")
    group_main = GROUP * CAP_MAIN
    group_rest = GROUP * 4

    loads = [
        pltpu.make_async_copy(w1_ref.at[0], w1.at[:, pl.ds(0, units)], local_sems.at[0]),
        pltpu.make_async_copy(w1_ref.at[1], w1.at[:, pl.ds(units, units)], local_sems.at[1]),
        pltpu.make_async_copy(w2_ref, w2, local_sems.at[2]),
    ]
    for load in loads:
        load.start()

    barrier = pltpu.get_barrier_semaphore()
    for axis in ("y", "z"):
        for way in (1, -1):
            pl.semaphore_signal(
                barrier, inc=1, device_id=seq_id(neighbour(axis, way)), device_id_type=MESH
            )
    for k in range(1, count):
        pl.semaphore_signal(
            barrier, inc=1, device_id=exp_id(lax.rem(e + k, count)), device_id_type=MESH
        )
    held, outs, sums = (held_a, held_b), (outs_a, outs_b), (sums_a, sums_b)
    held_a[0] = own_a[...]
    held_b[0] = own_b[...]
    pl.semaphore_wait(barrier, 4 + count - 1)

    def lanes(tree, part):
        total = 2 * mains[tree] + rests[tree]
        cut = total // 2 // LANES * LANES
        if part is None:
            return pl.ds(0, total)
        return pl.ds(0, cut) if part == 0 else pl.ds(cut, total - cut)

    def view_of(refs):
        return lambda tree, slot, part: refs[tree].at[slot, :, lanes(tree, part)]

    gather, gather_end = spread(view_of(held), send_sems, recv_sems)

    row = lax.broadcasted_iota(jnp.int32, (group_rest, group_rest * 4), 0)
    col = lax.broadcasted_iota(jnp.int32, (group_rest, group_rest * 4), 1)
    row_t = lax.broadcasted_iota(jnp.int32, (group_rest * 4, group_rest), 0)
    col_t = lax.broadcasted_iota(jnp.int32, (group_rest * 4, group_rest), 1)

    def pick(q):
        return one_hot(col == (row // 4) * 16 + q * 4 + row % 4)

    def put(q):
        return one_hot(row_t == (col_t // 4) * 16 + q * 4 + col_t % 4)

    half = width // 2
    members = GROUP * 16

    def feed(g):
        base = pl.ds(g * GROUP, GROUP)
        start = 0
        packed = []
        for tree in range(2):
            wide = mains[tree]
            for tile in range(2):
                rows_x[pl.ds(tile * members, members), pl.ds(start, wide)] = held[tree][
                    base, :, pl.ds(tile * wide, wide)
                ].reshape(members, wide)
            packed.append(
                held[tree][base, :, pl.ds(2 * wide, rests[tree])].reshape(members, rests[tree])
            )
            start += wide
        packed = jnp.concatenate(packed, axis=1)
        for q in range(4):
            rows_x[pl.ds(group_main, group_rest), pl.ds(q * quarter, quarter)] = dot(
                pick(q), packed
            ).astype(BF16)
        acc[...] = dot(rows_x[:, pl.ds(0, half)], w1[pl.ds(0, half), :])
        both = acc[...] + dot(rows_x[:, pl.ds(half, half)], w1[pl.ds(half, half), :])
        hidden[...] = (silu(both[:, :units]) * both[:, units:]).astype(BF16)

        start = 0
        for tree in range(2):
            wide = mains[tree]
            made = dot(hidden[...], w2[:, pl.ds(start, wide)]).astype(BF16)
            for tile in range(2):
                outs[tree][base, :, pl.ds(tile * wide, wide)] = made[
                    tile * members : (tile + 1) * members
                ].reshape(GROUP, 16, wide)
            few_acc[:, pl.ds(start, wide)] = made[group_main:]
            start += wide
        few = jnp.zeros((members, quarter), F32)
        for q in range(4):
            few = few + dot(put(q), few_acc[:, pl.ds(q * quarter, quarter)])
        few = few.astype(BF16)
        outs_a[base, :, pl.ds(2 * mains[0], rests[0])] = few[:, : rests[0]].reshape(
            GROUP, 16, rests[0]
        )
        outs_b[base, :, pl.ds(2 * mains[1], rests[1])] = few[:, rests[0] :].reshape(
            GROUP, 16, rests[1]
        )

    def when_full(g):
        if g == 0:
            for load in loads:
                load.wait()
        feed(g)

    gather(when_full)

    def add(tree, slot, child, part):
        here = lanes(tree, part)
        total = outs[tree][slot, :, here].astype(F32) + sums[tree][child, :, here].astype(F32)
        outs[tree][slot, :, here] = total.astype(BF16)

    reduce, reduce_end = gather_sum(
        view_of(outs), view_of(sums), add, sum_send_sems, sum_recv_sems
    )
    reduce()

    start = 0
    for tree in range(2):
        wide = mains[tree]
        for tile in range(2):
            made_rows[pl.ds(tile * 16, 16), pl.ds(start, wide)] = outs[tree][
                0, :, pl.ds(tile * wide, wide)
            ]
        start += wide
    packed = jnp.concatenate(
        [outs[tree][0, :, pl.ds(2 * mains[tree], rests[tree])] for tree in range(2)], axis=1
    )
    small_row = lax.broadcasted_iota(jnp.int32, (16, 16), 0)
    small_col = lax.broadcasted_iota(jnp.int32, (16, 16), 1)
    for q in range(4):
        choose = one_hot(jnp.logical_and(small_row < 4, small_col == q * 4 + small_row))
        made_rows[pl.ds(CAP_MAIN, 16), pl.ds(q * quarter, quarter)] = dot(choose, packed).astype(
            BF16
        )
    routes = routes_ref[...]
    gates = gate_ref[...]
    toks = routes.shape[0]
    table = slot_table(routes)
    mine_c = jnp.where(routes == e, gates, 0.0)
    weight = (mine_c[:, 0:1] + mine_c[:, 1:2]) * jnp.ones((1, LANES), F32)
    weight_t = weight.T
    lane = lax.broadcasted_iota(jnp.int32, (toks, LANES), 1)
    place = jnp.sum(jnp.where(lane == e, table, 0.0), axis=1, keepdims=True)
    place_t = (place * jnp.ones((1, LANES), F32)).T
    at = lax.broadcasted_iota(jnp.int32, (SLAB, toks), 0).astype(F32)
    mine = (at == place_t[0:1, :]).astype(F32)
    row_weight = jnp.sum(mine * weight_t[0:1, :], axis=1, keepdims=True)
    block = width // count
    for j in range(count):
        part = made_rows[:, pl.ds(j * block, block)].astype(F32)
        sent[j] = (row_weight * part).astype(BF16)

    def give(k):
        to = lax.rem(e + k, count)
        return pltpu.make_async_remote_copy(
            src_ref=sent.at[to],
            dst_ref=got.at[e],
            send_sem=out_send_sems.at[k - 1],
            recv_sem=out_recv_sems.at[k - 1],
            device_id=exp_id(to),
            device_id_type=MESH,
        )

    for k in range(1, count):
        give(k).start()
    got[e] = sent[e]
    for k in range(1, count):
        give(k).wait_recv()
    total = resid_ref[...]
    place_lane = lax.broadcasted_iota(jnp.int32, (toks, SLAB), 1).astype(F32)
    for j in range(count):
        total = total + dot(one_hot(place_lane == table[:, j : j + 1]), got[j])
    out_ref[...] = total.astype(BF16)

    gather_end()
    reduce_end()
    for k in range(1, count):
        give(k).wait_send()


def experts(own_a, own_b, resid, routes, gate_w, w1, w2):
    units, width = w2.shape
    count = lax.axis_size("exp")
    slots = len(SLOTS)
    sizes = [own_a.shape[1], own_b.shape[1]]
    group_rows = GROUP * (CAP_MAIN + 4)
    vmem = pl.BlockSpec(memory_space=pltpu.VMEM)
    hbm = pl.BlockSpec(memory_space=pl.ANY)
    return pl.pallas_call(
        experts_kernel,
        out_shape=jax.ShapeDtypeStruct(resid.shape, BF16),
        in_specs=[vmem] * 5 + [hbm, hbm],
        out_specs=vmem,
        scratch_shapes=[pltpu.VMEM((slots, 16, size), BF16) for _ in range(3) for size in sizes]
        + [
            pltpu.VMEM((width, 2 * units), BF16),
            pltpu.VMEM((units, width), BF16),
            pltpu.VMEM((group_rows, width), BF16),
            pltpu.VMEM((group_rows, 2 * units), F32),
            pltpu.VMEM((group_rows, units), BF16),
            pltpu.VMEM((GROUP * 4, width), BF16),
            pltpu.VMEM((SLAB, width), BF16),
            pltpu.VMEM((count, SLAB, width // count), BF16),
            pltpu.VMEM((count, SLAB, width // count), BF16),
            pltpu.SemaphoreType.DMA((3,)),
        ]
        + [pltpu.SemaphoreType.DMA((len(MESSAGES),)) for _ in range(4)]
        + [pltpu.SemaphoreType.DMA((count - 1,)) for _ in range(2)],
        compiler_params=pltpu.CompilerParams(
            collective_id=2, has_side_effects=True, vmem_limit_bytes=60 * 1024 * 1024
        ),
        name="experts",
    )(own_a, own_b, resid, routes, gate_w, w1, w2)


def shards(
    residual_in,
    mamba_in,
    bc_proj,
    decay,
    conv_w,
    mamba_vec,
    doc_len,
    w_out,
    norm_gain,
    routes,
    gate_w,
    w_gate_up,
    w_down,
):
    resid, own_a, own_b = mixer(
        mamba_in, bc_proj, decay, conv_w, mamba_vec, doc_len, residual_in, w_out, norm_gain, routes
    )
    return experts(own_a, own_b, resid, routes, gate_w, w_gate_up[0], w_down[0])


def solution(mesh):
    in_specs = (
        P("seq", None),
        P(None, "seq", "exp"),
        P(None, "seq"),
        P(None, "exp"),
        P(None, "exp"),
        P(None, "exp"),
        P(),
        P("exp", "seq"),
        P(),
        P("seq", None),
        P("seq", None),
        P("exp", None, None, "seq"),
        P("exp", "seq", None),
    )
    out_specs = P("seq", "exp")
    return jax.shard_map(shards, mesh=mesh, in_specs=in_specs, out_specs=out_specs, check_vma=False)
```

time: 1480 us -> 226 us (0.15); the launches traced: 1460 us -> 226 us
  other arithmetic: 398 us -> 0 us
  local copies, waits for them, and re-layouts: 389 us -> 8.48 us
  waiting for transfers between devices: 324 us -> 0 us
  Pallas kernels: 0 us -> 217 us
  starting transfers between devices: 174 us -> 0 us
  blocking collectives: 119 us -> 0 us
  matrix products: 35.4 us -> 0 us
    pallas_call x0 -> x2, Pallas kernels: none -> 217 us  [the longest x1 123 us: experts(): pl.pallas_call(experts_kernel, out_shape=jax.ShapeDtypeStruct(resid.shape...]
    dynamic_update_slice x128 -> x0, local copies, waits for them, and re-layouts: 177 us -> none  [shards(): lax.scan(advance, start, (step_size, u_values, b_rows, c_rows, keep))]
    dynamic_update_slice x128 -> x0, other arithmetic: 177 us -> none  [shards(): lax.scan(advance, start, (step_size, u_values, b_rows, c_rows, keep))]
    ppermute x32 -> x0, starting transfers between devices: 161 us -> none  [from_behind(): lax.ppermute(value, axis, [(source, source + steps) for source in range(i...]
    psum x1 -> x0, waiting for transfers between devices: 120 us -> none  [shards(): mix = lax.psum(partial_mix.astype(jnp.bfloat16), 'exp').astype(jnp.float32)]
    unnamed x1 -> x0, blocking collectives: 119 us -> none
    all_gather x2 -> x0, waiting for transfers between devices: 110 us -> none  [the longest x1 110 us: shards(): piece = lax.all_gather(sent_rows, 'seq', axis=0, tiled=True)]
    reduce_sum x132 -> x0, other arithmetic: 107 us -> none  [the longest x128 99.4 us: advance(): output = jnp.sum(state * c_row[:, None], axis=0)]
  transfers between devices with their start and end apart: 40 -> 0, of which waited for: 35 -> 0; matrix products, arithmetic and copies ran while one was open for 52% -> 0% of each run, Pallas kernels for 0% -> 0%
where the time goes in v1:
time: 226 us
  Pallas kernels  217 us (96%)
  local copies, waits for them, and re-layouts  8.48 us (4%)
    pallas_call x1, Pallas kernels, experts(): pl.pallas_call(experts_kernel, out_shape=jax.ShapeDtypeStruct(resid.shape...  123 us
    pallas_call x1, Pallas kernels, mixer(): pl.pallas_call(functools.partial(mixer_kernel, reach), out_shape=[jax.Sha...  94.6 us
    unnamed x6, local copies, waits for them, and re-layouts  8.48 us

profile of v1, /device:TPU:1, one launch (start us, length us, event | category | flops | bytes accessed | tf_op | source)
XLA Modules:
  0.0 226.0 jit_solution(13636108209417867525)
XLA Ops:
  0.0 1.3 copy.23
  1.3 1.3 copy.22
  2.6 1.4 copy.14.routes_ref
  4.0 1.5 copy.17
  5.5 1.4 copy.16.gate_ref
  6.9 94.6 %mixer.1 = (f32[128,512]{1,0:T(8,128)}, bf16[16,3712]{1,0:T(8,128)(2,1)}, bf16[16,5504]{1,0:T(8,128)(2,1)}) custom-call(bf16[3,128,1024]{2,1,0:T(8,128)(2,1)} %mamba_ref.1, f32[32,128]{1,0:T(8,128)} %bc_ref.1, f32[16,8,128]{2,1,0:T(8,128)} %bitcast.15, f32[4,8,128]{2,1,0:T(8,128)} %bitcast.16, f32[3,8,128]{2,1,0:T(8,128)} %bitcast.18, s32[8]{0:T(128)} %doc_ref.1, ...), custom_call_target="tpu_custom_call" | custom-call | tf_op jit(solution)/shard_map/mixer/pallas_call | solution.py:603
  101.5 122.9 %experts.1 = bf16[128,512]{1,0:T(8,128)(2,1)} custom-call(bf16[16,3712]{1,0:T(8,128)(2,1)} %get-tuple-element.8.own_a, bf16[16,5504]{1,0:T(8,128)(2,1)} %get-tuple-element.9.own_b, f32[128,512]{1,0:T(8,128)} %get-tuple-element.10.resid_ref, s32[128,2]{1,0:T(8,128)} %copy.14.routes_ref, f32[128,2]{1,0:T(8,128)} %copy.16.gate_ref, ...), custom_call_target="tpu_custom_call" | custom-call | tf_op jit(solution)/shard_map/experts/pallas_call | solution.py:879
  224.4 1.6 copy.25

commit v2 on v1

--- a/solution.py
+++ b/solution.py
@@ -1,5 +1,3 @@
-import functools
-
 import jax
 import jax.numpy as jnp
 from jax import lax
@@ -158,13 +156,13 @@
     return condition.astype(F32).astype(BF16)
 
 
-def slot_table(routes):
-    toks = routes.shape[0]
-    expert = lax.broadcasted_iota(jnp.int32, (toks, LANES), 1)
-    hits = jnp.logical_or(routes[:, 0:1] == expert, routes[:, 1:2] == expert)
+def slot_table(routes_t):
+    toks = routes_t.shape[1]
+    expert = lax.broadcasted_iota(jnp.int32, (LANES, toks), 0)
+    hits = jnp.logical_or(routes_t[0:1, :] == expert, routes_t[1:2, :] == expert)
     row = lax.broadcasted_iota(jnp.int32, (toks, toks), 0)
     col = lax.broadcasted_iota(jnp.int32, (toks, toks), 1)
-    places = dot(one_hot(col <= row), one_hot(hits)) - 1.0
+    places = dot(one_hot(hits), one_hot(row <= col)) - 1.0
     return jnp.where(hits, places, -1.0)
 
 
@@ -181,11 +179,11 @@
 
 
 CHUNKS = 4
-SHARES = [6, 12, 16, 22, 28, 34, 40, 46, 52, 60]
+SHARES = [6, 8, 10, 14, 18, 40, 50, 56, 62, 68]
+LATE_SHARES = [76, 84, 92, 98]
 
 
 def mixer_kernel(
-    reach,
     mamba_ref,
     bc_ref,
     decay_ref,
@@ -207,8 +205,8 @@
     tail,
     end_out,
     end_in,
-    sum_out,
-    sum_in,
+    start_out,
+    start_in,
     held_a,
     held_b,
     gated,
@@ -314,8 +312,16 @@
         reached[0] = stop
 
     forward(SHARES[0])
-    neg[...] = decay_ref[...] * (-LOG2E)
-    step_bias = vec_ref[1]
+    for j in range(blocks):
+        lanes = pl.ds(j * LANES, LANES)
+        neg[pl.ds(j, nstate, stride=rows), :] = decay_ref[:, lanes] * (-LOG2E)
+
+    def tile_row(ref, n):
+        return jnp.concatenate(
+            [ref[n : n + 1, j * LANES : (j + 1) * LANES] for j in range(blocks)], axis=0
+        )
+
+    step_bias = tile_row(vec_ref, 1)
 
     def tok(t):
         return pl.ds(pl.multiple_of(t * rows, rows), rows)
@@ -331,7 +337,7 @@
 
     forward(SHARES[1])
     tail_copy.wait()
-    there = jnp.where(me > 0, 1.0, 0.0).astype(F32)
+    there = jnp.where(me > 0, jnp.float32(1.0), jnp.float32(0.0))
     for j in range(blocks):
         rest = tail[:, pl.ds(j * LANES, LANES)].astype(F32) * there
         xs[pl.ds(j, 8, stride=rows), :] = rest[8:16, :]
@@ -348,13 +354,13 @@
             keep = jnp.where(end == position, jnp.float32(0.0), keep)
         return keep
 
-    taps = [conv_ref[k] for k in range(conv_ref.shape[0])]
-    conv_bias = vec_ref[0]
+    taps = [tile_row(conv_ref, k) for k in range(conv_ref.shape[0])]
+    conv_bias = tile_row(vec_ref, 0)
 
     def advance(t, states, keep, step, drive):
         new = []
         for n in range(nstate):
-            growth = jnp.exp2(step * neg[n]) * keep
+            growth = jnp.exp2(step * neg[pl.ds(n * rows, rows), :]) * keep
             new.append(growth * states[n] + drive * bc_ref[n, t])
         return tuple(new)
 
@@ -381,70 +387,94 @@
         if i < CHUNKS - 1:
             forward(SHARES[2 + i])
     states = carry[0]
+    high = total_step.astype(BF16)
+    low = (total_step - high.astype(F32)).astype(BF16)
     for n in range(0, nstate, 2):
-        pair = jnp.concatenate([states[n], states[n + 1]], axis=0)
-        end_out[pl.ds(n * rows, 2 * rows), :] = pair.astype(BF16)
-    sum_out[...] = total_step
-
-    def copies(k):
-        target = seq_id(lax.rem(me + k, count))
-        one = pltpu.make_async_remote_copy(
-            src_ref=end_out,
-            dst_ref=end_in.at[k - 1],
-            send_sem=send_sems.at[2 * k - 1],
-            recv_sem=recv_sems.at[2 * k - 1],
-            device_id=target,
+        pair = jnp.concatenate([states[n], states[n + 1]], axis=0).astype(BF16)
+        end_out[n // 2] = jnp.concatenate([pair, high, low], axis=0)
+    y, z = me // ZS, me % ZS
+    before = 2
+    end_in[before * ZS + z] = end_out[z]
+
+    def scatter(i):
+        row, step = i // ZS, i % ZS
+        holder = lax.rem(z + step, ZS)
+        return pltpu.make_async_remote_copy(
+            src_ref=end_out.at[holder],
+            dst_ref=end_in.at[(before - row) * ZS + z],
+            send_sem=send_sems.at[i],
+            recv_sem=recv_sems.at[i],
+            device_id=seq_id(lax.rem(y + row, YS) * ZS + holder),
             device_id_type=MESH,
         )
-        two = pltpu.make_async_remote_copy(
-            src_ref=sum_out,
-            dst_ref=sum_in.at[k - 1],
-            send_sem=send_sems.at[2 * k],
-            recv_sem=recv_sems.at[2 * k],
-            device_id=target,
+
+    def give_back(step):
+        return pltpu.make_async_remote_copy(
+            src_ref=start_out.at[lax.rem(z + step, ZS)],
+            dst_ref=start_in.at[z],
+            send_sem=send_sems.at[(before + 1) * ZS + step],
+            recv_sem=recv_sems.at[(before + 1) * ZS + step],
+            device_id=seq_id(y * ZS + lax.rem(z + step, ZS)),
             device_id_type=MESH,
         )
-        return one, two
-
-    def send(k, _):
-        one, two = copies(k)
-        one.start()
-        two.start()
+
+    def send(i, _):
+        scatter(i).start()
         return 0
 
-    lax.fori_loop(1, reach + 1, send, 0)
-
+    later = jnp.minimum(before + 1, YS - y) * ZS
+    earlier = jnp.minimum(before, y)
+    lax.fori_loop(1, later, send, 0)
     forward(SHARES[1 + CHUNKS])
 
-    def finish(k, _):
-        one, two = copies(k)
-        one.wait()
-        two.wait()
+    def arrive(i, _):
+        scatter(i).wait_recv()
         return 0
 
-    lax.fori_loop(1, reach + 1, finish, 0)
-
-    def enter(i, states):
-        k = reach - i
-        source = me - k
-        whole = jnp.where(source >= 0, jnp.float32(1.0), jnp.float32(0.0))
-        start = source * toks
-        unbroken = whole
+    lax.fori_loop(1, (earlier + 1) * ZS, arrive, 0)
+
+    def fold(at, held):
+        begin = ((y - before) * ZS + at) * toks
+        unbroken = jnp.float32(1.0)
         for end in ends:
-            inside = jnp.logical_and(end >= start, end < start + toks)
+            inside = jnp.logical_and(end >= begin, end < begin + toks)
             unbroken = jnp.where(inside, jnp.float32(0.0), unbroken)
-        sums = sum_in[k - 1]
+        halves = end_in[at, pl.ds(2 * rows, 2 * rows), :].astype(F32)
+        sums = halves[:rows] + halves[rows:]
+        pair = end_in[at, pl.ds(0, 2 * rows), :].astype(F32)
         new = []
-        for n in range(0, nstate, 2):
-            pair = end_in[k - 1, pl.ds(n * rows, 2 * rows), :].astype(F32)
-            for m in range(2):
-                growth = jnp.exp2(sums * neg[n + m]) * unbroken
-                new.append(growth * states[n + m] + whole * pair[m * rows : (m + 1) * rows, :])
+        for n in range(2):
+            rate = neg[pl.ds(pl.multiple_of((2 * z + n) * rows, rows), rows), :]
+            growth = jnp.exp2(sums * rate) * unbroken
+            new.append(growth * held[n] + pair[n * rows : (n + 1) * rows, :])
         return tuple(new)
 
-    entering = lax.fori_loop(0, reach, enter, zero)
+    def fold_own(at, held):
+        start_out[at - before * ZS] = jnp.concatenate(held, axis=0).astype(BF16)
+        return fold(at, held)
+
+    held = lax.fori_loop((before - earlier) * ZS, before * ZS, fold, zero[:2])
+    lax.fori_loop(before * ZS, (before + 1) * ZS, fold_own, held)
+
+    def return_start(step, _):
+        give_back(step).start()
+        return 0
+
+    lax.fori_loop(1, ZS, return_start, 0)
+    start_in[z] = start_out[z]
     forward(SHARES[2 + CHUNKS])
-    skip = vec_ref[2]
+
+    def return_arrive(step, _):
+        give_back(step).wait_recv()
+        return 0
+
+    lax.fori_loop(1, ZS, return_arrive, 0)
+    entering = []
+    for n in range(0, nstate, 2):
+        pair = start_in[n // 2].astype(F32)
+        entering += [pair[:rows], pair[rows:]]
+    entering = tuple(entering)
+    skip = tile_row(vec_ref, 2)
 
     def full_pass(t, states):
         keep = goes_on(first + t)
@@ -466,10 +496,10 @@
             forward(SHARES[3 + CHUNKS + i])
     for j in range(blocks):
         gated[:, pl.ds(j * LANES, LANES)] = zs[pl.ds(j, toks, stride=rows), :].astype(BF16)
-    for group in waiting:
+    for i, group in enumerate(list(waiting)):
         product(group)
-    routes = routes_ref[...]
-    table_t = slot_table(routes).T
+        forward(LATE_SHARES[i], act=True)
+    table_t = slot_table(routes_ref[...])
     forward(100, act=True)
 
     def pair_copy(k):
@@ -573,6 +603,17 @@
         start += wide
         rest_start += rests[tree]
 
+    def sent(i, _):
+        scatter(i).wait_send()
+        return 0
+
+    lax.fori_loop(1, later, sent, 0)
+
+    def returned(step, _):
+        give_back(step).wait_send()
+        return 0
+
+    lax.fori_loop(1, ZS, returned, 0)
     gather_end()
     for k in range(xs_count):
         pair_copy(k).wait_send()
@@ -587,7 +628,6 @@
     toks, channels = mamba_in.shape[1:]
     nstate = decay.shape[0]
     rows = channels // LANES
-    reach = 2048 // toks
     width = residual.shape[1]
     count = lax.axis_size("exp")
     block = width // count
@@ -597,11 +637,10 @@
     sizes = [2 * main + rest for main, rest in zip(mains, rests)]
     xs_count = count // CORES
     exp_sems = 2 * xs_count + 2 * (count - 1)
-    tiles = lambda a: a.reshape(a.shape[0], rows, LANES)
     vmem = pl.BlockSpec(memory_space=pltpu.VMEM)
     smem = pl.BlockSpec(memory_space=pltpu.SMEM)
     return pl.pallas_call(
-        functools.partial(mixer_kernel, reach),
+        mixer_kernel,
         out_shape=[jax.ShapeDtypeStruct((toks, block), F32)]
         + [jax.ShapeDtypeStruct((16, size), BF16) for size in sizes],
         in_specs=[vmem, smem, vmem, vmem, vmem, smem, vmem, vmem, vmem, vmem],
@@ -611,12 +650,12 @@
             pltpu.VMEM((toks * rows, LANES), F32),
             pltpu.VMEM((toks * rows, LANES), F32),
             pltpu.VMEM((toks * rows, LANES), F32),
-            pltpu.VMEM((nstate, rows, LANES), F32),
+            pltpu.VMEM((nstate * rows, LANES), F32),
             pltpu.VMEM((16, channels), BF16),
-            pltpu.VMEM((nstate * rows, LANES), BF16),
-            pltpu.VMEM((reach, nstate * rows, LANES), BF16),
-            pltpu.VMEM((rows, LANES), F32),
-            pltpu.VMEM((reach, rows, LANES), F32),
+            pltpu.VMEM((ZS, 4 * rows, LANES), BF16),
+            pltpu.VMEM((3 * ZS, 4 * rows, LANES), BF16),
+            pltpu.VMEM((ZS, 2 * rows, LANES), BF16),
+            pltpu.VMEM((ZS, 2 * rows, LANES), BF16),
             pltpu.VMEM((len(SLOTS), upper, LANES), BF16),
             pltpu.VMEM((len(SLOTS), depth - upper, LANES), BF16),
             pltpu.VMEM((toks, channels), BF16),
@@ -628,8 +667,8 @@
             pltpu.VMEM((count, SLAB, block), BF16),
             pltpu.VMEM((count, 8, LANES), F32),
             pltpu.VMEM((SLAB, width), BF16),
-            pltpu.SemaphoreType.DMA((2 * reach + 1,)),
-            pltpu.SemaphoreType.DMA((2 * reach + 1,)),
+            pltpu.SemaphoreType.DMA((4 * ZS,)),
+            pltpu.SemaphoreType.DMA((4 * ZS,)),
             pltpu.SemaphoreType.DMA((len(MESSAGES),)),
             pltpu.SemaphoreType.DMA((len(MESSAGES),)),
             pltpu.SemaphoreType.DMA((exp_sems,)),
@@ -642,9 +681,9 @@
     )(
         mamba_in,
         bc_proj,
-        tiles(decay),
-        tiles(conv_w),
-        tiles(mamba_vec),
+        decay,
+        conv_w,
+        mamba_vec,
         doc_len,
         residual,
         w_out,
@@ -822,19 +861,17 @@
         made_rows[pl.ds(CAP_MAIN, 16), pl.ds(q * quarter, quarter)] = dot(choose, packed).astype(
             BF16
         )
-    routes = routes_ref[...]
-    gates = gate_ref[...]
-    toks = routes.shape[0]
-    table = slot_table(routes)
-    mine_c = jnp.where(routes == e, gates, 0.0)
-    weight = (mine_c[:, 0:1] + mine_c[:, 1:2]) * jnp.ones((1, LANES), F32)
-    weight_t = weight.T
-    lane = lax.broadcasted_iota(jnp.int32, (toks, LANES), 1)
-    place = jnp.sum(jnp.where(lane == e, table, 0.0), axis=1, keepdims=True)
-    place_t = (place * jnp.ones((1, LANES), F32)).T
+    routes_t = routes_ref[...]
+    toks = routes_t.shape[1]
+    table_t = slot_table(routes_t)
+    table = table_t.T
+    chosen = jnp.where(routes_t == e, gate_ref[...], 0.0)
+    weight_t = chosen[0:1, :] + chosen[1:2, :]
+    expert_row = lax.broadcasted_iota(jnp.int32, (LANES, toks), 0)
+    place_t = jnp.sum(jnp.where(expert_row == e, table_t, 0.0), axis=0, keepdims=True)
     at = lax.broadcasted_iota(jnp.int32, (SLAB, toks), 0).astype(F32)
-    mine = (at == place_t[0:1, :]).astype(F32)
-    row_weight = jnp.sum(mine * weight_t[0:1, :], axis=1, keepdims=True)
+    mine = (at == place_t).astype(F32)
+    row_weight = jnp.sum(mine * weight_t, axis=1, keepdims=True)
     block = width // count
     for j in range(count):
         part = made_rows[:, pl.ds(j * block, block)].astype(F32)
@@ -919,9 +956,18 @@
     w_down,
 ):
     resid, own_a, own_b = mixer(
-        mamba_in, bc_proj, decay, conv_w, mamba_vec, doc_len, residual_in, w_out, norm_gain, routes
+        mamba_in,
+        bc_proj,
+        decay,
+        conv_w,
+        mamba_vec,
+        doc_len,
+        residual_in,
+        w_out,
+        norm_gain,
+        routes.T,
     )
-    return experts(own_a, own_b, resid, routes, gate_w, w_gate_up[0], w_down[0])
+    return experts(own_a, own_b, resid, routes.T, gate_w.T, w_gate_up[0], w_down[0])
 
 
 def solution(mesh):

time: 226 us -> 211 us (0.934)
  Pallas kernels: 217 us -> 209 us
  local copies, waits for them, and re-layouts: 8.48 us -> 1.57 us
    pallas_call x1, Pallas kernels: 94.6 us -> 86.1 us  [mixer(): pl.pallas_call(mixer_kernel, out_shape=[jax.ShapeDtypeStruct((toks, block...]
    unnamed x6 -> x1, local copies, waits for them, and re-layouts: 8.48 us -> 1.57 us
where the time goes in v2:
time: 211 us
  Pallas kernels  209 us (99%)
    pallas_call x1, Pallas kernels, experts(): pl.pallas_call(experts_kernel, out_shape=jax.ShapeDtypeStruct(resid.shape...  123 us
    pallas_call x1, Pallas kernels, mixer(): pl.pallas_call(mixer_kernel, out_shape=[jax.ShapeDtypeStruct((toks, block...  86.1 us

profile of v2, /device:TPU:1, one launch (start us, length us, event | category | flops | bytes accessed | tf_op | source)
XLA Modules:
  0.0 211.0 jit_solution(13638584096853378162)
XLA Ops:
  0.0 86.1 %mixer.1 = (f32[128,512]{1,0:T(8,128)}, bf16[16,3712]{1,0:T(8,128)(2,1)}, bf16[16,5504]{1,0:T(8,128)(2,1)}) custom-call(bf16[3,128,1024]{2,1,0:T(8,128)(2,1)} %mamba_ref.1, f32[32,128]{1,0:T(8,128)} %bc_ref.1, f32[16,1024]{1,0:T(8,128)} %decay_ref.1, f32[4,1024]{1,0:T(4,128)} %conv_ref.1, f32[3,1024]{1,0:T(4,128)} %vec_ref.1, s32[8]{0:T(128)} %doc_ref.1, ...), custom_call_target="tpu_custom_call" | custom-call | tf_op jit(solution)/shard_map/mixer/pallas_call | solution.py:642
  86.1 123.3 %experts.1 = bf16[128,512]{1,0:T(8,128)(2,1)} custom-call(bf16[16,3712]{1,0:T(8,128)(2,1)} %get-tuple-element.8.own_a, bf16[16,5504]{1,0:T(8,128)(2,1)} %get-tuple-element.9.own_b, f32[128,512]{1,0:T(8,128)} %get-tuple-element.10.resid_ref, s32[2,128]{1,0:T(2,128)} %bitcast.9, f32[2,128]{1,0:T(2,128)} %bitcast.10, bf16[2,4096,384]{2,1,0:T(8,128)(2,1)} %bitcast.5, ...), custom_call_target="tpu_custom_call" | custom-call | tf_op jit(solution)/shard_map/experts/pallas_call | solution.py:916
  209.4 1.6 copy.15

commit v3 on v2

--- a/solution.py
+++ b/solution.py
@@ -178,9 +178,17 @@
     return (first, width - first), (rest, quarter - rest)
 
 
-CHUNKS = 4
-SHARES = [6, 8, 10, 14, 18, 40, 50, 56, 62, 68]
-LATE_SHARES = [76, 84, 92, 98]
+def ring_steps(offsets, size):
+    return [
+        (offset, to, way, part)
+        for offset in offsets
+        for to, way, part in far_steps(offset, size)
+    ]
+
+
+W_SLOTS = Z_OFFSETS
+W_STEPS = ring_steps(Z_OFFSETS, ZS)
+GATED_STEPS = ring_steps(Y_OFFSETS, YS)
 
 
 def mixer_kernel(
@@ -207,8 +215,7 @@
     end_in,
     start_out,
     start_in,
-    held_a,
-    held_b,
+    held_w,
     gated,
     partial,
     pair_in,
@@ -218,10 +225,18 @@
     disp_in,
     squares,
     rows_n,
+    mix_out,
+    mix_in,
+    final_out,
+    final_in,
     send_sems,
     recv_sems,
     w_send_sems,
     w_recv_sems,
+    g_send_sems,
+    g_recv_sems,
+    y_send_sems,
+    y_recv_sems,
     exp_send_sems,
     exp_recv_sems,
 ):
@@ -255,9 +270,8 @@
         )
 
     depth = w_ref.shape[0]
-    upper = held_a.shape[1]
-    held_a[0] = w_ref[pl.ds(0, upper), :]
-    held_b[0] = w_ref[pl.ds(upper, depth - upper), :]
+    held_w[0] = w_ref[...]
+    y, z = me // ZS, me % ZS
     for j in range(blocks):
         lanes = pl.ds(j * LANES, LANES)
         xs[pl.ds(8 * rows + j, toks, stride=rows), :] = mamba_ref[0, :, lanes].astype(F32)
@@ -265,14 +279,33 @@
         dts[pl.ds(j, toks, stride=rows), :] = mamba_ref[2, :, lanes].astype(F32)
     pl.semaphore_wait(barrier, count - 1 + experts_count - 1)
 
-    def held_view(tree, slot, part):
-        ref = (held_a, held_b)[tree]
-        size = ref.shape[1]
-        if part is None:
-            return ref.at[slot]
-        return ref.at[slot, pl.ds(part * (size // 2), size // 2)]
-
-    gather, gather_end = spread(held_view, w_send_sems, w_recv_sems)
+    flows = 2
+    flow_rows = depth // flows
+
+    def w_copy(k, flow):
+        source, target, way, part = W_STEPS[k]
+        size = flow_rows if part is None else flow_rows // 2
+        here = pl.ds(flow * flow_rows + (part or 0) * size, size)
+        return pltpu.make_async_remote_copy(
+            src_ref=held_w.at[W_SLOTS.index(source), here],
+            dst_ref=held_w.at[W_SLOTS.index(target), here],
+            send_sem=w_send_sems.at[k * flows + flow],
+            recv_sem=w_recv_sems.at[k * flows + flow],
+            device_id=seq_id(neighbour("z", way)),
+            device_id_type=MESH,
+        )
+
+    def forward(round):
+        for flow in range(flows):
+            for way in (1, -1):
+                for k, step in enumerate(W_STEPS):
+                    if step[2] == way and abs(step[0]) == round - 1:
+                        w_copy(k, flow).wait_recv()
+                for k, step in enumerate(W_STEPS):
+                    if step[2] == way and abs(step[0]) == round:
+                        w_copy(k, flow).start()
+
+
     tail_copy = pltpu.make_async_remote_copy(
         src_ref=mamba_ref.at[0, pl.ds(toks - 16, 16)],
         dst_ref=tail,
@@ -283,35 +316,7 @@
     )
     tail_copy.start()
 
-    waiting = []
-    reached = [0]
-
-    def product(group):
-        for pair in range(GROUP // 2):
-            first_slot = group * GROUP + 2 * pair
-            sides = [
-                jnp.concatenate([held_a[first_slot + n], held_b[first_slot + n]], axis=0)
-                for n in range(2)
-            ]
-            made = dot(gated[...], jnp.concatenate(sides, axis=1)).astype(BF16)
-            for n in range(2):
-                dy, dz = SLOTS[first_slot + n]
-                y, z = me // ZS, me % ZS
-                owner = ((y - dy + YS) % YS) * ZS + (z - dz + ZS) % ZS
-                block = owner // tiles_per
-                lane = pl.multiple_of((owner % tiles_per) * LANES, LANES)
-                partial[block % CORES, block // CORES, :, pl.ds(lane, LANES)] = made[
-                    :, n * LANES : (n + 1) * LANES
-                ]
-
-    tiles_per = resid_ref.shape[1] // LANES
-
-    def forward(share, act=False):
-        stop = len(ORDER) * share // 100
-        gather(product if act else waiting.append, reached[0], stop)
-        reached[0] = stop
-
-    forward(SHARES[0])
+    forward(0)
     for j in range(blocks):
         lanes = pl.ds(j * LANES, LANES)
         neg[pl.ds(j, nstate, stride=rows), :] = decay_ref[:, lanes] * (-LOG2E)
@@ -335,7 +340,6 @@
 
     total_step = lax.fori_loop(0, toks, prepare, jnp.zeros((rows, LANES), F32), unroll=8)
 
-    forward(SHARES[1])
     tail_copy.wait()
     there = jnp.where(me > 0, jnp.float32(1.0), jnp.float32(0.0))
     for j in range(blocks):
@@ -380,19 +384,12 @@
 
     zero = tuple(jnp.zeros((rows, LANES), F32) for _ in range(nstate))
     carry = (zero, goes_on(first - 1), goes_on(first - 2))
-    for i in range(CHUNKS):
-        carry = lax.fori_loop(
-            i * toks // CHUNKS, (i + 1) * toks // CHUNKS, local_pass, carry, unroll=2
-        )
-        if i < CHUNKS - 1:
-            forward(SHARES[2 + i])
-    states = carry[0]
+    states, _, _ = lax.fori_loop(0, toks, local_pass, carry, unroll=2)
     high = total_step.astype(BF16)
     low = (total_step - high.astype(F32)).astype(BF16)
     for n in range(0, nstate, 2):
         pair = jnp.concatenate([states[n], states[n + 1]], axis=0).astype(BF16)
         end_out[n // 2] = jnp.concatenate([pair, high, low], axis=0)
-    y, z = me // ZS, me % ZS
     before = 2
     end_in[before * ZS + z] = end_out[z]
 
@@ -425,7 +422,7 @@
     later = jnp.minimum(before + 1, YS - y) * ZS
     earlier = jnp.minimum(before, y)
     lax.fori_loop(1, later, send, 0)
-    forward(SHARES[1 + CHUNKS])
+    forward(1)
 
     def arrive(i, _):
         scatter(i).wait_recv()
@@ -462,7 +459,7 @@
 
     lax.fori_loop(1, ZS, return_start, 0)
     start_in[z] = start_out[z]
-    forward(SHARES[2 + CHUNKS])
+    forward(2)
 
     def return_arrive(step, _):
         give_back(step).wait_recv()
@@ -487,20 +484,61 @@
         zs[tok(t), :] = zs[tok(t), :] * total
         return states
 
+    half = toks // 2
+
+    def gated_copy(k, piece):
+        source, target, way, part = GATED_STEPS[k]
+        size = half if part is None else half // 2
+        here = pl.ds(piece * half + (part or 0) * size, size)
+        return pltpu.make_async_remote_copy(
+            src_ref=gated.at[Y_OFFSETS.index(source), here],
+            dst_ref=gated.at[Y_OFFSETS.index(target), here],
+            send_sem=g_send_sems.at[k * 2 + piece],
+            recv_sem=g_recv_sems.at[k * 2 + piece],
+            device_id=seq_id(neighbour("y", way)),
+            device_id_type=MESH,
+        )
+
     states = entering
-    for i in range(CHUNKS):
-        states = lax.fori_loop(
-            i * toks // CHUNKS, (i + 1) * toks // CHUNKS, full_pass, states, unroll=2
-        )
-        if i < CHUNKS - 1:
-            forward(SHARES[3 + CHUNKS + i])
-    for j in range(blocks):
-        gated[:, pl.ds(j * LANES, LANES)] = zs[pl.ds(j, toks, stride=rows), :].astype(BF16)
-    for i, group in enumerate(list(waiting)):
-        product(group)
-        forward(LATE_SHARES[i], act=True)
+    for piece in range(2):
+        states = lax.fori_loop(piece * half, (piece + 1) * half, full_pass, states, unroll=2)
+        for j in range(blocks):
+            gated[0, pl.ds(piece * half, half), pl.ds(j * LANES, LANES)] = zs[
+                pl.ds(piece * half * rows + j, half, stride=rows), :
+            ].astype(BF16)
+        for k, step in enumerate(GATED_STEPS):
+            if step[0] == 0:
+                gated_copy(k, piece).start()
+    forward(3)
     table_t = slot_table(routes_ref[...])
-    forward(100, act=True)
+
+    def product(slots):
+        left = jnp.concatenate([gated[i] for i in slots], axis=0)
+        for pair in range(ZS // 2):
+            right = jnp.concatenate([held_w[2 * pair], held_w[2 * pair + 1]], axis=1)
+            made = dot(left, right).astype(BF16)
+            for n in range(2):
+                owner = (z - W_SLOTS[2 * pair + n] + ZS) % ZS
+                for i, slot in enumerate(slots):
+                    shard = (y - Y_OFFSETS[slot] + YS) % YS
+                    partial[owner % CORES, owner // CORES, shard] = made[
+                        i * toks : (i + 1) * toks, n * LANES : (n + 1) * LANES
+                    ]
+
+    for piece in range(2):
+        for k, step in enumerate(GATED_STEPS):
+            if step[0] == 0:
+                gated_copy(k, piece).wait_recv()
+                for k2, step2 in enumerate(GATED_STEPS):
+                    if step2[0] == step[1]:
+                        gated_copy(k2, piece).start()
+    forward(4)
+    product([0, 1, 2])
+    for piece in range(2):
+        for k, step in enumerate(GATED_STEPS):
+            if step[0] != 0:
+                gated_copy(k, piece).wait_recv()
+    product([3])
 
     def pair_copy(k):
         to = lax.rem(x + k, xs_count)
@@ -534,13 +572,57 @@
         if k > 0:
             pair_sum[to] = total.astype(BF16)
             cross_copy(k).start()
-    width = residual_ref.shape[1]
-    block = width // experts_count
-    total = total + residual_ref[:, pl.ds(pl.multiple_of(e * block, block), block)].astype(F32)
     for k in (1, 3, 2):
         cross_copy(k).wait_recv()
         total = total + cross_in[k - 1].astype(F32)
-    resid_ref[...] = total
+
+    mix_out[...] = total.astype(BF16)
+
+    def shard_copy(k):
+        to = lax.rem(y + k, YS)
+        return pltpu.make_async_remote_copy(
+            src_ref=mix_out.at[to],
+            dst_ref=mix_in.at[y],
+            send_sem=y_send_sems.at[k - 1],
+            recv_sem=y_recv_sems.at[k - 1],
+            device_id=seq_id(to * ZS + z),
+            device_id_type=MESH,
+        )
+
+    for k in (2, 1, 3):
+        shard_copy(k).start()
+    mix_in[y] = mix_out[y]
+    for k in (1, 3, 2):
+        shard_copy(k).wait_recv()
+    width = residual_ref.shape[1]
+    block = width // experts_count
+    quarter = width // YS
+    sides = []
+    for q in range(YS):
+        lane = pl.multiple_of(q * quarter + e * LANES, LANES)
+        sides.append(residual_ref[:, pl.ds(lane, LANES)].astype(F32) + mix_in[q].astype(F32))
+        final_out[q] = sides[q].astype(BF16)
+    total = jnp.concatenate(sides, axis=1)
+
+    def final_copy(q):
+        return pltpu.make_async_remote_copy(
+            src_ref=final_out.at[q],
+            dst_ref=final_in.at[e % YS],
+            send_sem=y_send_sems.at[YS - 1 + q],
+            recv_sem=y_recv_sems.at[YS - 1 + e % YS],
+            device_id=exp_id(CORES * q + e // YS),
+            device_id_type=MESH,
+        )
+
+    def final_wait(j):
+        return pltpu.make_async_remote_copy(
+            src_ref=final_out.at[0],
+            dst_ref=final_in.at[j],
+            send_sem=y_send_sems.at[YS - 1],
+            recv_sem=y_recv_sems.at[YS - 1 + j],
+            device_id=exp_id(lax.rem(e + 1, experts_count)),
+            device_id_type=MESH,
+        )
 
     square = jnp.sum(total * total, axis=1, keepdims=True)
     squares[e] = (square * jnp.ones((1, LANES), F32)).T[0:8, :]
@@ -568,6 +650,17 @@
     for k in range(1, experts_count):
         for copy in deal(k):
             copy.start()
+    for q in range(YS):
+        home = CORES * q + e // YS == e
+
+        @pl.when(home)
+        def _():
+            final_in[e % YS] = final_out[q]
+
+        @pl.when(jnp.logical_not(home))
+        def _():
+            final_copy(q).start()
+
     disp_in[e] = disp[e]
     expert_row = lax.broadcasted_iota(jnp.int32, (LANES, toks), 0)
     place_t = jnp.sum(jnp.where(expert_row == e, table_t, 0.0), axis=0, keepdims=True)
@@ -582,10 +675,11 @@
     inverse = lax.rsqrt(mean * (1.0 / width) + 1e-05)
     scale = jnp.sum(mine * inverse[0:1, :], axis=1, keepdims=True)
     for j in range(experts_count):
-        here = pl.ds(j * block, block)
-        rows_n[:, here] = (disp_in[j].astype(F32) * scale * gain_ref[:, here]).astype(BF16)
+        for q in range(YS):
+            here = pl.ds(q * quarter + j * LANES, LANES)
+            dealt = disp_in[j, :, pl.ds(q * LANES, LANES)].astype(F32)
+            rows_n[:, here] = (dealt * scale * gain_ref[:, here]).astype(BF16)
     mains, rests = split_lanes(width)
-    quarter = width // 4
     small_row = lax.broadcasted_iota(jnp.int32, (16, 16), 0)
     small_col = lax.broadcasted_iota(jnp.int32, (16, 16), 1)
     packed = jnp.zeros((16, quarter), F32)
@@ -603,6 +697,29 @@
         start += wide
         rest_start += rests[tree]
 
+    for j in range(YS):
+        source = (e % CORES) * YS + j
+
+        @pl.when(source != e)
+        def _():
+            final_wait(j).wait_recv()
+
+        resid_ref[:, pl.ds(j * LANES, LANES)] = final_in[j].astype(F32)
+    for q in range(YS):
+
+        @pl.when(CORES * q + e // YS != e)
+        def _():
+            final_copy(q).wait_send()
+
+    for k in range(1, YS):
+        shard_copy(k).wait_send()
+    for k in range(len(GATED_STEPS)):
+        for piece in range(2):
+            gated_copy(k, piece).wait_send()
+    for k in range(len(W_STEPS)):
+        for flow in range(flows):
+            w_copy(k, flow).wait_send()
+
     def sent(i, _):
         scatter(i).wait_send()
         return 0
@@ -614,7 +731,6 @@
         return 0
 
     lax.fori_loop(1, ZS, returned, 0)
-    gather_end()
     for k in range(xs_count):
         pair_copy(k).wait_send()
         if k > 0:
@@ -632,7 +748,6 @@
     count = lax.axis_size("exp")
     block = width // count
     depth = w_out.shape[0]
-    upper = depth * 13 // 32 // 32 * 32
     mains, rests = split_lanes(width)
     sizes = [2 * main + rest for main, rest in zip(mains, rests)]
     xs_count = count // CORES
@@ -656,21 +771,28 @@
             pltpu.VMEM((3 * ZS, 4 * rows, LANES), BF16),
             pltpu.VMEM((ZS, 2 * rows, LANES), BF16),
             pltpu.VMEM((ZS, 2 * rows, LANES), BF16),
-            pltpu.VMEM((len(SLOTS), upper, LANES), BF16),
-            pltpu.VMEM((len(SLOTS), depth - upper, LANES), BF16),
-            pltpu.VMEM((toks, channels), BF16),
-            pltpu.VMEM((CORES, xs_count, toks, block), BF16),
-            pltpu.VMEM((xs_count, toks, block), BF16),
-            pltpu.VMEM((xs_count, toks, block), BF16),
-            pltpu.VMEM((xs_count - 1, toks, block), BF16),
+            pltpu.VMEM((ZS, depth, LANES), BF16),
+            pltpu.VMEM((YS, toks, channels), BF16),
+            pltpu.VMEM((CORES, xs_count, YS, toks, LANES), BF16),
+            pltpu.VMEM((xs_count, YS, toks, LANES), BF16),
+            pltpu.VMEM((xs_count, YS, toks, LANES), BF16),
+            pltpu.VMEM((xs_count - 1, YS, toks, LANES), BF16),
             pltpu.VMEM((count, SLAB, block), BF16),
             pltpu.VMEM((count, SLAB, block), BF16),
             pltpu.VMEM((count, 8, LANES), F32),
             pltpu.VMEM((SLAB, width), BF16),
+            pltpu.VMEM((YS, toks, LANES), BF16),
+            pltpu.VMEM((YS, toks, LANES), BF16),
+            pltpu.VMEM((YS, toks, LANES), BF16),
+            pltpu.VMEM((YS, toks, LANES), BF16),
             pltpu.SemaphoreType.DMA((4 * ZS,)),
             pltpu.SemaphoreType.DMA((4 * ZS,)),
-            pltpu.SemaphoreType.DMA((len(MESSAGES),)),
-            pltpu.SemaphoreType.DMA((len(MESSAGES),)),
+            pltpu.SemaphoreType.DMA((2 * len(W_STEPS),)),
+            pltpu.SemaphoreType.DMA((2 * len(W_STEPS),)),
+            pltpu.SemaphoreType.DMA((2 * len(GATED_STEPS),)),
+            pltpu.SemaphoreType.DMA((2 * len(GATED_STEPS),)),
+            pltpu.SemaphoreType.DMA((2 * YS - 1,)),
+            pltpu.SemaphoreType.DMA((2 * YS - 1,)),
             pltpu.SemaphoreType.DMA((exp_sems,)),
             pltpu.SemaphoreType.DMA((exp_sems,)),
         ],

time: 211 us -> 198 us (0.938)
  Pallas kernels: 209 us -> 196 us
    pallas_call x1, Pallas kernels: 86.1 us -> 73.4 us  [mixer(): pl.pallas_call(mixer_kernel, out_shape=[jax.ShapeDtypeStruct((toks, block...]
where the time goes in v3:
time: 198 us
  Pallas kernels  196 us (99%)
    pallas_call x1, Pallas kernels, experts(): pl.pallas_call(experts_kernel, out_shape=jax.ShapeDtypeStruct(resid.shape...  123 us
    pallas_call x1, Pallas kernels, mixer(): pl.pallas_call(mixer_kernel, out_shape=[jax.ShapeDtypeStruct((toks, block...  73.4 us

profile of v3, /device:TPU:1, one launch (start us, length us, event | category | flops | bytes accessed | tf_op | source)
XLA Modules:
  0.0 197.8 jit_solution(9212820595265450756)
XLA Ops:
  0.0 73.4 %mixer.1 = (f32[128,512]{1,0:T(8,128)}, bf16[16,3712]{1,0:T(8,128)(2,1)}, bf16[16,5504]{1,0:T(8,128)(2,1)}) custom-call(bf16[3,128,1024]{2,1,0:T(8,128)(2,1)} %mamba_ref.1, f32[32,128]{1,0:T(8,128)} %bc_ref.1, f32[16,1024]{1,0:T(8,128)} %decay_ref.1, f32[4,1024]{1,0:T(4,128)} %conv_ref.1, f32[3,1024]{1,0:T(4,128)} %vec_ref.1, s32[8]{0:T(128)} %doc_ref.1, ...), custom_call_target="tpu_custom_call" | custom-call | tf_op jit(solution)/shard_map/mixer/pallas_call | solution.py:757
  73.4 122.8 %experts.1 = bf16[128,512]{1,0:T(8,128)(2,1)} custom-call(bf16[16,3712]{1,0:T(8,128)(2,1)} %get-tuple-element.8.own_a, bf16[16,5504]{1,0:T(8,128)(2,1)} %get-tuple-element.9.own_b, f32[128,512]{1,0:T(8,128)} %get-tuple-element.10.resid_ref, s32[2,128]{1,0:T(2,128)} %bitcast.9, f32[2,128]{1,0:T(2,128)} %bitcast.10, bf16[2,4096,384]{2,1,0:T(8,128)(2,1)} %bitcast.5, ...), custom_call_target="tpu_custom_call" | custom-call | tf_op jit(solution)/shard_map/experts/pallas_call | solution.py:1038
  196.2 1.6 copy.15

commit v4 on v3

--- a/solution.py
+++ b/solution.py
@@ -191,7 +191,7 @@
 GATED_STEPS = ring_steps(Y_OFFSETS, YS)
 
 
-def mixer_kernel(
+def mixer_part(
     mamba_ref,
     bc_ref,
     decay_ref,
@@ -416,7 +416,7 @@
         )
 
     def send(i, _):
-        scatter(i).start()
+        scatter(later - i).start()
         return 0
 
     later = jnp.minimum(before + 1, YS - y) * ZS
@@ -697,126 +697,54 @@
         start += wide
         rest_start += rests[tree]
 
-    for j in range(YS):
-        source = (e % CORES) * YS + j
-
-        @pl.when(source != e)
-        def _():
-            final_wait(j).wait_recv()
-
-        resid_ref[:, pl.ds(j * LANES, LANES)] = final_in[j].astype(F32)
-    for q in range(YS):
-
-        @pl.when(CORES * q + e // YS != e)
-        def _():
-            final_copy(q).wait_send()
-
-    for k in range(1, YS):
-        shard_copy(k).wait_send()
-    for k in range(len(GATED_STEPS)):
-        for piece in range(2):
-            gated_copy(k, piece).wait_send()
-    for k in range(len(W_STEPS)):
-        for flow in range(flows):
-            w_copy(k, flow).wait_send()
-
-    def sent(i, _):
-        scatter(i).wait_send()
-        return 0
-
-    lax.fori_loop(1, later, sent, 0)
-
-    def returned(step, _):
-        give_back(step).wait_send()
-        return 0
-
-    lax.fori_loop(1, ZS, returned, 0)
-    for k in range(xs_count):
-        pair_copy(k).wait_send()
-        if k > 0:
-            cross_copy(k).wait_send()
-    for k in range(1, experts_count):
-        for copy in deal(k):
-            copy.wait_send()
-
-
-def mixer(mamba_in, bc_proj, decay, conv_w, mamba_vec, doc_len, residual, w_out, gain, routes):
-    toks, channels = mamba_in.shape[1:]
-    nstate = decay.shape[0]
-    rows = channels // LANES
-    width = residual.shape[1]
-    count = lax.axis_size("exp")
-    block = width // count
-    depth = w_out.shape[0]
-    mains, rests = split_lanes(width)
-    sizes = [2 * main + rest for main, rest in zip(mains, rests)]
-    xs_count = count // CORES
-    exp_sems = 2 * xs_count + 2 * (count - 1)
-    vmem = pl.BlockSpec(memory_space=pltpu.VMEM)
-    smem = pl.BlockSpec(memory_space=pltpu.SMEM)
-    return pl.pallas_call(
-        mixer_kernel,
-        out_shape=[jax.ShapeDtypeStruct((toks, block), F32)]
-        + [jax.ShapeDtypeStruct((16, size), BF16) for size in sizes],
-        in_specs=[vmem, smem, vmem, vmem, vmem, smem, vmem, vmem, vmem, vmem],
-        out_specs=[vmem] * 3,
-        scratch_shapes=[
-            pltpu.VMEM(((toks + 8) * rows, LANES), F32),
-            pltpu.VMEM((toks * rows, LANES), F32),
-            pltpu.VMEM((toks * rows, LANES), F32),
-            pltpu.VMEM((toks * rows, LANES), F32),
-            pltpu.VMEM((nstate * rows, LANES), F32),
-            pltpu.VMEM((16, channels), BF16),
-            pltpu.VMEM((ZS, 4 * rows, LANES), BF16),
-            pltpu.VMEM((3 * ZS, 4 * rows, LANES), BF16),
-            pltpu.VMEM((ZS, 2 * rows, LANES), BF16),
-            pltpu.VMEM((ZS, 2 * rows, LANES), BF16),
-            pltpu.VMEM((ZS, depth, LANES), BF16),
-            pltpu.VMEM((YS, toks, channels), BF16),
-            pltpu.VMEM((CORES, xs_count, YS, toks, LANES), BF16),
-            pltpu.VMEM((xs_count, YS, toks, LANES), BF16),
-            pltpu.VMEM((xs_count, YS, toks, LANES), BF16),
-            pltpu.VMEM((xs_count - 1, YS, toks, LANES), BF16),
-            pltpu.VMEM((count, SLAB, block), BF16),
-            pltpu.VMEM((count, SLAB, block), BF16),
-            pltpu.VMEM((count, 8, LANES), F32),
-            pltpu.VMEM((SLAB, width), BF16),
-            pltpu.VMEM((YS, toks, LANES), BF16),
-            pltpu.VMEM((YS, toks, LANES), BF16),
-            pltpu.VMEM((YS, toks, LANES), BF16),
-            pltpu.VMEM((YS, toks, LANES), BF16),
-            pltpu.SemaphoreType.DMA((4 * ZS,)),
-            pltpu.SemaphoreType.DMA((4 * ZS,)),
-            pltpu.SemaphoreType.DMA((2 * len(W_STEPS),)),
-            pltpu.SemaphoreType.DMA((2 * len(W_STEPS),)),
-            pltpu.SemaphoreType.DMA((2 * len(GATED_STEPS),)),
-            pltpu.SemaphoreType.DMA((2 * len(GATED_STEPS),)),
-            pltpu.SemaphoreType.DMA((2 * YS - 1,)),
-            pltpu.SemaphoreType.DMA((2 * YS - 1,)),
-            pltpu.SemaphoreType.DMA((exp_sems,)),
-            pltpu.SemaphoreType.DMA((exp_sems,)),
-        ],
-        compiler_params=pltpu.CompilerParams(
-            collective_id=1, has_side_effects=True, vmem_limit_bytes=56 * 1024 * 1024
-        ),
-        name="mixer",
-    )(
-        mamba_in,
-        bc_proj,
-        decay,
-        conv_w,
-        mamba_vec,
-        doc_len,
-        residual,
-        w_out,
-        gain.reshape(1, width),
-        routes,
-    )
-
-
-def experts_kernel(
-    own_a,
-    own_b,
+    def finish():
+        for j in range(YS):
+            source = (e % CORES) * YS + j
+
+            @pl.when(source != e)
+            def _():
+                final_wait(j).wait_recv()
+
+            resid_ref[:, pl.ds(j * LANES, LANES)] = final_in[j].astype(F32)
+        for q in range(YS):
+
+            @pl.when(CORES * q + e // YS != e)
+            def _():
+                final_copy(q).wait_send()
+
+        for k in range(1, YS):
+            shard_copy(k).wait_send()
+        for k in range(len(GATED_STEPS)):
+            for piece in range(2):
+                gated_copy(k, piece).wait_send()
+        for k in range(len(W_STEPS)):
+            for flow in range(flows):
+                w_copy(k, flow).wait_send()
+
+        def sent(i, _):
+            scatter(i).wait_send()
+            return 0
+
+        lax.fori_loop(1, later, sent, 0)
+
+        def returned(step, _):
+            give_back(step).wait_send()
+            return 0
+
+        lax.fori_loop(1, ZS, returned, 0)
+        for k in range(xs_count):
+            pair_copy(k).wait_send()
+            if k > 0:
+                cross_copy(k).wait_send()
+        for k in range(1, experts_count):
+            for copy in deal(k):
+                copy.wait_send()
+
+    return finish
+
+
+def experts_part(
+    mixer_end,
     resid_ref,
     routes_ref,
     gate_ref,
@@ -862,20 +790,7 @@
     for load in loads:
         load.start()
 
-    barrier = pltpu.get_barrier_semaphore()
-    for axis in ("y", "z"):
-        for way in (1, -1):
-            pl.semaphore_signal(
-                barrier, inc=1, device_id=seq_id(neighbour(axis, way)), device_id_type=MESH
-            )
-    for k in range(1, count):
-        pl.semaphore_signal(
-            barrier, inc=1, device_id=exp_id(lax.rem(e + k, count)), device_id_type=MESH
-        )
     held, outs, sums = (held_a, held_b), (outs_a, outs_b), (sums_a, sums_b)
-    held_a[0] = own_a[...]
-    held_b[0] = own_b[...]
-    pl.semaphore_wait(barrier, 4 + count - 1)
 
     def lanes(tree, part):
         total = 2 * mains[tree] + rests[tree]
@@ -1015,6 +930,7 @@
     got[e] = sent[e]
     for k in range(1, count):
         give(k).wait_recv()
+    mixer_end()
     total = resid_ref[...]
     place_lane = lax.broadcasted_iota(jnp.int32, (toks, SLAB), 1).astype(F32)
     for j in range(count):
@@ -1027,20 +943,117 @@
         give(k).wait_send()
 
 
-def experts(own_a, own_b, resid, routes, gate_w, w1, w2):
+def layer_kernel(
+    mamba_ref,
+    bc_ref,
+    decay_ref,
+    conv_ref,
+    vec_ref,
+    doc_ref,
+    residual_ref,
+    w_ref,
+    gain_ref,
+    routes_ref,
+    gate_ref,
+    w1_ref,
+    w2_ref,
+    out_ref,
+    resid,
+    held_a,
+    held_b,
+    *scratch,
+):
+    mixer_refs, expert_refs = scratch[:MIXER_SCRATCH], scratch[MIXER_SCRATCH:]
+    mixer_end = mixer_part(
+        mamba_ref,
+        bc_ref,
+        decay_ref,
+        conv_ref,
+        vec_ref,
+        doc_ref,
+        residual_ref,
+        w_ref,
+        gain_ref,
+        routes_ref,
+        resid,
+        held_a.at[0],
+        held_b.at[0],
+        *mixer_refs,
+    )
+    experts_part(
+        mixer_end,
+        resid,
+        routes_ref,
+        gate_ref,
+        w1_ref,
+        w2_ref,
+        out_ref,
+        held_a,
+        held_b,
+        *expert_refs,
+    )
+
+
+MIXER_SCRATCH = 34
+
+
+def layer(mamba_in, bc, decay, conv_w, vec, doc_len, residual, w_out, gain, routes, gates, w1, w2):
+    toks, channels = mamba_in.shape[1:]
+    nstate = decay.shape[0]
+    rows = channels // LANES
     units, width = w2.shape
     count = lax.axis_size("exp")
-    slots = len(SLOTS)
-    sizes = [own_a.shape[1], own_b.shape[1]]
+    block = width // count
+    depth = w_out.shape[0]
+    mains, rests = split_lanes(width)
+    sizes = [2 * main + rest for main, rest in zip(mains, rests)]
+    xs_count = count // CORES
+    exp_sems = 2 * xs_count + 2 * (count - 1)
     group_rows = GROUP * (CAP_MAIN + 4)
     vmem = pl.BlockSpec(memory_space=pltpu.VMEM)
+    smem = pl.BlockSpec(memory_space=pltpu.SMEM)
     hbm = pl.BlockSpec(memory_space=pl.ANY)
-    return pl.pallas_call(
-        experts_kernel,
-        out_shape=jax.ShapeDtypeStruct(resid.shape, BF16),
-        in_specs=[vmem] * 5 + [hbm, hbm],
-        out_specs=vmem,
-        scratch_shapes=[pltpu.VMEM((slots, 16, size), BF16) for _ in range(3) for size in sizes]
+    held = [pltpu.VMEM((len(SLOTS), 16, size), BF16) for size in sizes]
+    mixer_scratch = [
+        pltpu.VMEM(((toks + 8) * rows, LANES), F32),
+        pltpu.VMEM((toks * rows, LANES), F32),
+        pltpu.VMEM((toks * rows, LANES), F32),
+        pltpu.VMEM((toks * rows, LANES), F32),
+        pltpu.VMEM((nstate * rows, LANES), F32),
+        pltpu.VMEM((16, channels), BF16),
+        pltpu.VMEM((ZS, 4 * rows, LANES), BF16),
+        pltpu.VMEM((3 * ZS, 4 * rows, LANES), BF16),
+        pltpu.VMEM((ZS, 2 * rows, LANES), BF16),
+        pltpu.VMEM((ZS, 2 * rows, LANES), BF16),
+        pltpu.VMEM((ZS, depth, LANES), BF16),
+        pltpu.VMEM((YS, toks, channels), BF16),
+        pltpu.VMEM((CORES, xs_count, YS, toks, LANES), BF16),
+        pltpu.VMEM((xs_count, YS, toks, LANES), BF16),
+        pltpu.VMEM((xs_count, YS, toks, LANES), BF16),
+        pltpu.VMEM((xs_count - 1, YS, toks, LANES), BF16),
+        pltpu.VMEM((count, SLAB, block), BF16),
+        pltpu.VMEM((count, SLAB, block), BF16),
+        pltpu.VMEM((count, 8, LANES), F32),
+        pltpu.VMEM((SLAB, width), BF16),
+        pltpu.VMEM((YS, toks, LANES), BF16),
+        pltpu.VMEM((YS, toks, LANES), BF16),
+        pltpu.VMEM((YS, toks, LANES), BF16),
+        pltpu.VMEM((YS, toks, LANES), BF16),
+        pltpu.SemaphoreType.DMA((4 * ZS,)),
+        pltpu.SemaphoreType.DMA((4 * ZS,)),
+        pltpu.SemaphoreType.DMA((2 * len(W_STEPS),)),
+        pltpu.SemaphoreType.DMA((2 * len(W_STEPS),)),
+        pltpu.SemaphoreType.DMA((2 * len(GATED_STEPS),)),
+        pltpu.SemaphoreType.DMA((2 * len(GATED_STEPS),)),
+        pltpu.SemaphoreType.DMA((2 * YS - 1,)),
+        pltpu.SemaphoreType.DMA((2 * YS - 1,)),
+        pltpu.SemaphoreType.DMA((exp_sems,)),
+        pltpu.SemaphoreType.DMA((exp_sems,)),
+    ]
+    assert len(mixer_scratch) == MIXER_SCRATCH
+    expert_scratch = (
+        held
+        + held
         + [
             pltpu.VMEM((width, 2 * units), BF16),
             pltpu.VMEM((units, width), BF16),
@@ -1049,17 +1062,38 @@
             pltpu.VMEM((group_rows, units), BF16),
             pltpu.VMEM((GROUP * 4, width), BF16),
             pltpu.VMEM((SLAB, width), BF16),
-            pltpu.VMEM((count, SLAB, width // count), BF16),
-            pltpu.VMEM((count, SLAB, width // count), BF16),
+            pltpu.VMEM((count, SLAB, block), BF16),
+            pltpu.VMEM((count, SLAB, block), BF16),
             pltpu.SemaphoreType.DMA((3,)),
         ]
         + [pltpu.SemaphoreType.DMA((len(MESSAGES),)) for _ in range(4)]
-        + [pltpu.SemaphoreType.DMA((count - 1,)) for _ in range(2)],
+        + [pltpu.SemaphoreType.DMA((count - 1,)) for _ in range(2)]
+    )
+    return pl.pallas_call(
+        layer_kernel,
+        out_shape=jax.ShapeDtypeStruct((toks, block), BF16),
+        in_specs=[vmem, smem, vmem, vmem, vmem, smem, vmem, vmem, vmem, vmem, vmem, hbm, hbm],
+        out_specs=vmem,
+        scratch_shapes=[pltpu.VMEM((toks, block), F32)] + held + mixer_scratch + expert_scratch,
         compiler_params=pltpu.CompilerParams(
-            collective_id=2, has_side_effects=True, vmem_limit_bytes=60 * 1024 * 1024
+            collective_id=1, has_side_effects=True, vmem_limit_bytes=62 * 1024 * 1024
         ),
-        name="experts",
-    )(own_a, own_b, resid, routes, gate_w, w1, w2)
+        name="layer",
+    )(
+        mamba_in,
+        bc,
+        decay,
+        conv_w,
+        vec,
+        doc_len,
+        residual,
+        w_out,
+        gain.reshape(1, width),
+        routes,
+        gates,
+        w1,
+        w2,
+    )
 
 
 def shards(
@@ -1077,7 +1111,7 @@
     w_gate_up,
     w_down,
 ):
-    resid, own_a, own_b = mixer(
+    return layer(
         mamba_in,
         bc_proj,
         decay,
@@ -1088,8 +1122,10 @@
         w_out,
         norm_gain,
         routes.T,
+        gate_w.T,
+        w_gate_up[0],
+        w_down[0],
     )
-    return experts(own_a, own_b, resid, routes.T, gate_w.T, w_gate_up[0], w_down[0])
 
 
 def solution(mesh):

time: 198 us -> 194 us (0.980)
  Pallas kernels: 196 us -> 192 us
    pallas_call x2 -> x1, Pallas kernels: 196 us -> 192 us  [layer(): pl.pallas_call(layer_kernel, out_shape=jax.ShapeDtypeStruct((toks, block)...]
where the time goes in v4:
time: 194 us
  Pallas kernels  192 us (99%)
    pallas_call x1, Pallas kernels, layer(): pl.pallas_call(layer_kernel, out_shape=jax.ShapeDtypeStruct((toks, block)...  192 us

profile of v4, /device:TPU:1, one launch (start us, length us, event | category | flops | bytes accessed | tf_op | source)
XLA Modules:
  0.0 193.9 jit_solution(10198898528857351043)
XLA Ops:
  0.0 192.3 %layer.1 = bf16[128,512]{1,0:T(8,128)(2,1)} custom-call(bf16[3,128,1024]{2,1,0:T(8,128)(2,1)} %mamba_ref.1, f32[32,128]{1,0:T(8,128)} %bc_ref.1, f32[16,1024]{1,0:T(8,128)} %decay_ref.1, f32[4,1024]{1,0:T(4,128)} %conv_ref.1, f32[3,1024]{1,0:T(4,128)} %vec_ref.1, s32[8]{0:T(128)} %doc_ref.1, bf16[128,4096]{1,0:T(8,128)(2,1)} %residual_ref.1, ...), custom_call_target="tpu_custom_call" | custom-call | tf_op jit(solution)/shard_map/layer/pallas_call | solution.py:1072
  192.3 1.6 copy.15

commit v5 on v4

--- a/solution.py
+++ b/solution.py
@@ -384,7 +384,7 @@
 
     zero = tuple(jnp.zeros((rows, LANES), F32) for _ in range(nstate))
     carry = (zero, goes_on(first - 1), goes_on(first - 2))
-    states, _, _ = lax.fori_loop(0, toks, local_pass, carry, unroll=2)
+    states, _, _ = lax.fori_loop(0, toks, local_pass, carry, unroll=4)
     high = total_step.astype(BF16)
     low = (total_step - high.astype(F32)).astype(BF16)
     for n in range(0, nstate, 2):
@@ -501,7 +501,7 @@
 
     states = entering
     for piece in range(2):
-        states = lax.fori_loop(piece * half, (piece + 1) * half, full_pass, states, unroll=2)
+        states = lax.fori_loop(piece * half, (piece + 1) * half, full_pass, states, unroll=4)
         for j in range(blocks):
             gated[0, pl.ds(piece * half, half), pl.ds(j * LANES, LANES)] = zs[
                 pl.ds(piece * half * rows + j, half, stride=rows), :
@@ -745,6 +745,7 @@
 
 def experts_part(
     mixer_end,
+    loads,
     resid_ref,
     routes_ref,
     gate_ref,
@@ -782,14 +783,6 @@
     group_main = GROUP * CAP_MAIN
     group_rest = GROUP * 4
 
-    loads = [
-        pltpu.make_async_copy(w1_ref.at[0], w1.at[:, pl.ds(0, units)], local_sems.at[0]),
-        pltpu.make_async_copy(w1_ref.at[1], w1.at[:, pl.ds(units, units)], local_sems.at[1]),
-        pltpu.make_async_copy(w2_ref, w2, local_sems.at[2]),
-    ]
-    for load in loads:
-        load.start()
-
     held, outs, sums = (held_a, held_b), (outs_a, outs_b), (sums_a, sums_b)
 
     def lanes(tree, part):
@@ -928,17 +921,17 @@
     for k in range(1, count):
         give(k).start()
     got[e] = sent[e]
+    gather_end()
+    mixer_end()
+    reduce_end()
     for k in range(1, count):
         give(k).wait_recv()
-    mixer_end()
     total = resid_ref[...]
     place_lane = lax.broadcasted_iota(jnp.int32, (toks, SLAB), 1).astype(F32)
     for j in range(count):
         total = total + dot(one_hot(place_lane == table[:, j : j + 1]), got[j])
     out_ref[...] = total.astype(BF16)
 
-    gather_end()
-    reduce_end()
     for k in range(1, count):
         give(k).wait_send()
 
@@ -964,6 +957,15 @@
     *scratch,
 ):
     mixer_refs, expert_refs = scratch[:MIXER_SCRATCH], scratch[MIXER_SCRATCH:]
+    w1, w2, local_sems = expert_refs[4], expert_refs[5], expert_refs[13]
+    units = w2_ref.shape[0]
+    loads = [
+        pltpu.make_async_copy(w1_ref.at[0], w1.at[:, pl.ds(0, units)], local_sems.at[0]),
+        pltpu.make_async_copy(w1_ref.at[1], w1.at[:, pl.ds(units, units)], local_sems.at[1]),
+        pltpu.make_async_copy(w2_ref, w2, local_sems.at[2]),
+    ]
+    for load in loads:
+        load.start()
     mixer_end = mixer_part(
         mamba_ref,
         bc_ref,
@@ -982,6 +984,7 @@
     )
     experts_part(
         mixer_end,
+        loads,
         resid,
         routes_ref,
         gate_ref,

time: 194 us -> 192 us (0.990)
  no operation moved by 1% of the time
where the time goes in v5:
time: 192 us
  Pallas kernels  191 us (99%)
    pallas_call x1, Pallas kernels, layer(): pl.pallas_call(layer_kernel, out_shape=jax.ShapeDtypeStruct((toks, block)...  191 us

profile of v5, /device:TPU:1, one launch (start us, length us, event | category | flops | bytes accessed | tf_op | source)
XLA Modules:
  0.0 192.3 jit_solution(15099777903475686238)
XLA Ops:
  0.0 190.7 %layer.1 = bf16[128,512]{1,0:T(8,128)(2,1)} custom-call(bf16[3,128,1024]{2,1,0:T(8,128)(2,1)} %mamba_ref.1, f32[32,128]{1,0:T(8,128)} %bc_ref.1, f32[16,1024]{1,0:T(8,128)} %decay_ref.1, f32[4,1024]{1,0:T(4,128)} %conv_ref.1, f32[3,1024]{1,0:T(4,128)} %vec_ref.1, s32[8]{0:T(128)} %doc_ref.1, bf16[128,4096]{1,0:T(8,128)(2,1)} %residual_ref.1, ...), custom_call_target="tpu_custom_call" | custom-call | tf_op jit(solution)/shard_map/layer/pallas_call | solution.py:1075
  190.7 1.6 copy.15
